TPU v7x, 32 devices: a whole 2x2x4 slice. The times are simulated.
32 devices in a mesh: expert: 16 (over z, y, x), dp: 2 (over core).
Axes of the slice: x: 2, y: 2, z: 4, core: 2. Of those that a mesh axis runs over, the one named last changes fastest.
Arguments:
- tokens: bfloat16 [768, 2048], P(('expert', 'dp')), may hold values from -6 to 6
- expert_ids: int32 [768, 8], P(('expert', 'dp')), may hold values from 0 to 15, all different within a row; in each aligned block of 24 rows (0 to 23, 24 to 47, ...) at most 16 rows name the same one
- route_weight: float32 [768, 8], P(('expert', 'dp')), may hold values from 0.05 to 0.5
- cotangent: bfloat16 [768, 2048], P(('expert', 'dp')), may hold values from -6 to 6
- holder: int32 [16], replicated, may hold values from 0 to 15, each once
- partner: int32 [16], replicated, may hold values from 0 to 15, as said below
- up_weight: bfloat16 [16, 2048, 768], P('expert', 'dp'), may hold values from -0.125 to 0.125
- down_weight: bfloat16 [16, 768, 2048], P('expert', None, 'dp'), may hold values from -0.21875 to 0.21875
- up_moment: bfloat16 [16, 2048, 768], P('expert', 'dp'), may hold values from -1.796875 to 1.796875
- down_moment: bfloat16 [16, 768, 2048], P('expert', None, 'dp'), may hold values from -1.796875 to 1.796875
Outputs:
- layer_out: bfloat16 [768, 2048], P(('expert', 'dp'))
- up_moment_new: bfloat16 [16, 2048, 768], P('expert', 'dp')
- down_moment_new: bfloat16 [16, 768, 2048], P('expert', None, 'dp')
Inputs may be any that keep to these rules, and one draw needn't show every extreme that they name: `expert_ids`: each token names 8 different experts; within each device's block of 24 tokens no expert is named by more than 16 tokens, a bound that some block reaches. `holder`: A permutation of the slots. partner[partner[s]] = s for every slot s, and exactly 2 * (4) slots have partner[s] != s.
All inputs are finite; a program needn't handle non-finite values.
Results may differ from a plain program's by a relative error of at most 0.022.
Values may be sent and summed in bfloat16 or wider, within the bound.
A program may use at most 128 MiB of HBM per device.

v0:
```python
import jax
import jax.numpy as jnp
from jax import lax
from jax.sharding import PartitionSpec as P

MOMENT_DECAY = 0.9


def silu_slope(preact):
    sigmoid_value = jax.nn.sigmoid(preact)
    return sigmoid_value * (1.0 + preact * (1.0 - sigmoid_value))


def swap_slots(arrays, partner, slot_count):
    stacked = jnp.stack([array_item.reshape(slot_count, -1) for array_item in arrays], axis=1)
    spread = lax.all_to_all(stacked, "expert", split_axis=0, concat_axis=0, tiled=True)
    picked = jnp.take(spread, partner, axis=0)
    landed = lax.all_to_all(picked, "expert", split_axis=0, concat_axis=0, tiled=True)
    return [landed[:, member].reshape(array_item.shape) for member, array_item in enumerate(arrays)]


def body(
    tokens,
    expert_ids,
    route_weight,
    cotangent,
    holder,
    partner,
    up_weight,
    down_weight,
    up_moment,
    down_moment,
):
    tok_count, top_count = expert_ids.shape
    n_slots = lax.axis_size("expert")
    n_groups = lax.axis_size("dp")
    capacity = min(tok_count, max(2, 4 * tok_count * top_count // (3 * n_slots)))
    feature_count = tokens.shape[1]
    quarter = feature_count // n_groups
    slot_range = jnp.arange(n_slots, dtype=jnp.int32)
    held_hit = (holder[:, None] == slot_range[None, :]).astype(jnp.int32)
    target = jnp.sum(held_hit * partner[None, :], axis=1)
    swapped = swap_slots([up_weight, down_weight, up_moment, down_moment], partner, n_slots)
    up_weight, down_weight, up_moment, down_moment = (
        swapped[0],
        swapped[1],
        swapped[2],
        swapped[3],
    )
    flat_ids = expert_ids.reshape(-1)
    expert_hit = (flat_ids[:, None] == slot_range[None, :]).astype(jnp.int32)
    destination = jnp.sum(expert_hit * target[None, :], axis=1)
    dest_hit = (destination[:, None] == slot_range[None, :]).astype(jnp.int32)
    position = jnp.sum((jnp.cumsum(dest_hit, axis=0) - 1) * dest_hit, axis=1)
    entry_index = destination * capacity + position
    slots_total = n_slots * capacity
    select = (jnp.arange(slots_total, dtype=jnp.int32)[:, None] == entry_index[None, :]).reshape(
        slots_total, tok_count, top_count
    )
    picked = jnp.sum(select.astype(jnp.float32), axis=2)
    scaled = jnp.sum(jnp.where(select, route_weight[None, :, :], 0.0), axis=2)
    sent_rows = jnp.dot(
        picked.astype(jnp.bfloat16), tokens, preferred_element_type=jnp.float32
    ).astype(jnp.bfloat16)
    sent_grads = jnp.dot(
        scaled,
        cotangent.astype(jnp.float32),
        precision=lax.Precision.HIGHEST,
        preferred_element_type=jnp.float32,
    ).astype(jnp.bfloat16)
    outgoing = jnp.stack([sent_rows, sent_grads], axis=0).reshape(
        1, 2, n_slots, capacity, feature_count
    )
    arrived = lax.all_to_all(
        lax.all_to_all(outgoing, "expert", split_axis=2, concat_axis=2, tiled=True),
        "dp",
        split_axis=4,
        concat_axis=0,
        tiled=True,
    )
    rows_in = arrived[:, 0].reshape(-1, quarter)
    grads_in = arrived[:, 1].reshape(-1, quarter)
    up_local = up_weight[0]
    down_local = down_weight[0]
    pre_part = jnp.dot(rows_in, up_local, preferred_element_type=jnp.float32)
    back_part = lax.dot_general(
        grads_in, down_local, (((1,), (1,)), ((), ())), preferred_element_type=jnp.float32
    )
    preact, back_sum = (
        lax.psum(pre_part.astype(jnp.bfloat16), "dp").astype(jnp.float32),
        lax.psum(back_part.astype(jnp.bfloat16), "dp").astype(jnp.float32),
    )
    hidden = jax.nn.silu(preact).astype(jnp.bfloat16)
    pre_grad = (back_sum * silu_slope(preact)).astype(jnp.bfloat16)
    out_part = jnp.dot(hidden, down_local, preferred_element_type=jnp.float32).astype(jnp.bfloat16)
    up_grad = lax.dot_general(
        rows_in, pre_grad, (((0,), (0,)), ((), ())), preferred_element_type=jnp.float32
    )
    down_grad = lax.dot_general(
        hidden, grads_in, (((0,), (0,)), ((), ())), preferred_element_type=jnp.float32
    )
    returned = lax.all_to_all(
        lax.all_to_all(
            out_part.reshape(n_groups, n_slots, capacity, quarter),
            "expert",
            split_axis=1,
            concat_axis=1,
            tiled=True,
        ),
        "dp",
        split_axis=0,
        concat_axis=3,
        tiled=True,
    )
    layer_out = jnp.dot(
        scaled.T,
        returned.reshape(slots_total, feature_count).astype(jnp.float32),
        precision=lax.Precision.HIGHEST,
        preferred_element_type=jnp.float32,
    ).astype(jnp.bfloat16)
    new_up = (
        MOMENT_DECAY * up_moment.astype(jnp.float32) + (1.0 - MOMENT_DECAY) * up_grad[None]
    ).astype(jnp.bfloat16)
    new_down = (
        MOMENT_DECAY * down_moment.astype(jnp.float32) + (1.0 - MOMENT_DECAY) * down_grad[None]
    ).astype(jnp.bfloat16)
    return (layer_out, new_up, new_down)


def solution(mesh):
    return jax.shard_map(
        body,
        mesh=mesh,
        in_specs=(
            P(("expert", "dp"), None),
            P(("expert", "dp"), None),
            P(("expert", "dp"), None),
            P(("expert", "dp"), None),
            P(),
            P(),
            P("expert", "dp", None),
            P("expert", None, "dp"),
            P("expert", "dp", None),
            P("expert", None, "dp"),
        ),
        out_specs=(P(("expert", "dp"), None), P("expert", "dp", None), P("expert", None, "dp")),
        check_vma=False,
    )
```

profile of v0, /device:TPU:0, one launch (start us, length us, event | category | flops | bytes accessed | tf_op | source)
XLA Modules:
  0.0 494.7 jit_solution(16086205135713134854)
XLA Ops:
  7.2 0.0 copy-start
  7.2 0.8 copy.62
  8.0 0.1 eq.63
  8.1 0.9 select_reduce_fusion.2
  8.9 0.1 select_reduce_fusion.1
  9.0 0.6 reduce-window.6
  9.6 0.2 slice_reduce_fusion.2
  9.9 0.1 bitcast_bitcast_fusion
  10.0 0.1 add.36
  10.1 0.8 copy.65
  10.8 0.2 convert_reduce_fusion
  11.0 0.0 copy-done
  11.0 1.0 convolution_convert_fusion.1
  12.1 1.3 convolution_convert_fusion
  13.4 1.5 pad_maximum_fusion.1
  14.9 8.4 %all-to-all-start = ((bf16[1,2,16,16,2048]{4,3,1,0,2:T(8,128)(2,1)}), bf16[1,2,16,16,2048]{4,3,1,0,2:T(8,128)(2,1)}, u32[]{:S(2)}, u32[]{:S(2)}) async-start(bf16[1,2,16,16,2048]{4,3,1,0,2:T(8,128)(2,1)} %pad_maximum_fusion.1), calls=%async_computation | async-start | bytes 4194304 | tf_op jit(solution)/shard_map/all_to_all | solution.py:75
  23.3 4.2 stack_reshape.16
  27.5 6.2 %stack_reshape.17 = bf16[16,1,49152]{2,1,0:T(2,128)(2,1)} reshape(bf16[1,768,1024]{2,1,0:T(8,128)(2,1)} %param.17) | data formatting | bytes 3145728 | tf_op jit(solution)/shard_map/stack;reshape | solution.py:15
  33.8 5.9 %stack_reshape.18 = bf16[16,1,49152]{2,1,0:T(2,128)(2,1)} reshape(bf16[1,1024,768]{2,1,0:T(8,128)(2,1)} %param.18) | data formatting | bytes 3145728 | tf_op jit(solution)/shard_map/stack;reshape | solution.py:15
  39.7 6.2 %stack_reshape.19 = bf16[16,1,49152]{2,1,0:T(2,128)(2,1)} reshape(bf16[1,768,1024]{2,1,0:T(8,128)(2,1)} %param.19) | data formatting | bytes 3145728 | tf_op jit(solution)/shard_map/stack;reshape | solution.py:15
  45.9 17.1 %pad_maximum_fusion = bf16[16,4,49152]{2,1,0:T(4,128)(2,1)} fusion(bf16[16,1,49152]{2,1,0:T(2,128)(2,1)} %stack_reshape.19, bf16[16,1,49152]{2,1,0:T(2,128)(2,1)} %stack_reshape.18, bf16[16,1,49152]{2,1,0:T(2,128)(2,1)} %stack_reshape.17, bf16[16,1,49152]{2,1,0:T(2,128)(2,1)S(1)} %stack_reshape.16), kind=kLoop, calls=%fused_computation.1 | loop fusion | flops 25165824 | bytes 12582912 | tf_op jit(solution)/shard_map/stack | solution.py:15
  62.9 3.5 all-to-all-done
  66.4 10.2 %all-to-all-start.2 = ((bf16[16,4,49152]{2,1,0:T(4,128)(2,1)}), bf16[16,4,49152]{2,1,0:T(4,128)(2,1)}, u32[]{:S(2)}, u32[]{:S(2)}) async-start(bf16[16,4,49152]{2,1,0:T(4,128)(2,1)} %pad_maximum_fusion), calls=%async_computation.2 | async-start | bytes 12582912 | tf_op jit(solution)/shard_map/all_to_all | solution.py:16
  76.6 0.0 copy-done.9
  76.7 23.4 %copy.68 = bf16[1,2,16,16,2048]{3,2,1,0,4:T(8,128)(2,1)} copy(bf16[1,2,16,16,2048]{4,3,1,0,2:T(8,128)(2,1)} %all-to-all-done) | data formatting | bytes 4194304 | tf_op jit(solution)/shard_map/all_to_all | solution.py:75
  100.1 26.0 %reshape.97 = bf16[2,2,262144]{2,1,0:T(2,128)(2,1)} reshape(bf16[2048,1,2,16,16]{4,3,2,1,0:T(8,128)(2,1)} %bitcast.50) | data formatting | bytes 4194304
  126.1 66.7 %all-to-all-done.2 = bf16[16,4,49152]{2,1,0:T(4,128)(2,1)} async-done(((bf16[16,4,49152]{2,1,0:T(4,128)(2,1)}), bf16[16,4,49152]{2,1,0:T(4,128)(2,1)}, u32[]{:S(2)}, u32[]{:S(2)}) %all-to-all-start.2) | async-done | bytes 6291488 | tf_op jit(solution)/shard_map/all_to_all | solution.py:16
  192.8 4.0 all-to-all-start.1
  196.8 10.3 %gather_fusion = bf16[16,4,49152]{2,1,0:T(4,128)(2,1)} fusion(bf16[16,4,49152]{2,1,0:T(4,128)(2,1)} %all-to-all-done.2, s32[1024]{0:T(1024)S(1)} %pad_clamp_fusion), kind=kCustom, calls=%fused_computation | custom fusion | bytes 12582976 | tf_op jit(solution)/shard_map/jit(_take)/gather | solution.py:17
  207.0 8.2 %broadcast_select_fusion = bf16[16,4,49152]{2,1,0:T(4,128)(2,1)} fusion(bf16[16,4,49152]{2,1,0:T(4,128)(2,1)} %gather_fusion, pred[16]{0:T(512)(128)(4,1)S(1)} %compare_and_fusion), kind=kLoop, calls=%fused_computation.2 | loop fusion | flops 3145728 | bytes 12582928 | tf_op jit(solution)/shard_map/jit(_take)/select_n | solution.py:17
  215.2 0.0 all-to-all-done.1
  215.2 28.6 %all-to-all-start.3 = ((bf16[16,4,49152]{2,1,0:T(4,128)(2,1)}), bf16[16,4,49152]{2,1,0:T(4,128)(2,1)}, u32[]{:S(2)}, u32[]{:S(2)}) async-start(bf16[16,4,49152]{2,1,0:T(4,128)(2,1)} %broadcast_select_fusion), calls=%async_computation.3 | async-start | bytes 12582912 | tf_op jit(solution)/shard_map/all_to_all | solution.py:18
  243.9 0.4 all-reduce.4.cloned.1.call-start
  244.4 17.7 %reshape.98 = bf16[2048,1,2,16,16]{4,3,2,1,0:T(8,128)(2,1)} reshape(bf16[2,2,262144]{2,1,0:T(2,128)(2,1)S(1)} %all-to-all-done.1) | data formatting | bytes 4194304
  262.0 17.6 %copy.79 = bf16[1,2,16,16,2,1024]{5,4,3,2,1,0:T(2,128)(2,1)S(1)} copy(bf16[1,2,16,16,2,1024]{3,2,1,5,4,0:T(8,128)(2,1)} %bitcast.51) | data formatting | bytes 4194304 | tf_op jit(solution)/shard_map/all_to_all | solution.py:74
  279.6 1.6 fusion.22
  281.2 1.3 copy.78
  282.5 1.3 copy.70
  283.8 80.4 %all-to-all-done.3 = bf16[16,4,49152]{2,1,0:T(4,128)(2,1)} async-done(((bf16[16,4,49152]{2,1,0:T(4,128)(2,1)}), bf16[16,4,49152]{2,1,0:T(4,128)(2,1)}, u32[]{:S(2)}, u32[]{:S(2)}) %all-to-all-start.3) | async-done | bytes 6291488 | tf_op jit(solution)/shard_map/all_to_all | solution.py:18
  364.2 15.4 %slice_reduce_fusion.1 = (bf16[16,49152]{1,0:T(8,128)(2,1)S(1)}, bf16[16,49152]{1,0:T(8,128)(2,1)S(1)}) fusion(bf16[16,4,49152]{2,1,0:T(4,128)(2,1)} %all-to-all-done.3), kind=kLoop, calls=%fused_computation.10 | loop fusion | bytes 6291456 | tf_op jit(solution)/shard_map/slice | solution.py:19
  379.6 1.6 squeeze_reshape_squeeze.7
  381.2 1.8 squeeze_reshape_squeeze.6
  383.0 0.0 copy-start.4
  383.0 0.0 copy-start.5
  383.0 3.3 convolution_convert_fusion.4
  386.3 0.0 copy-done.5
  386.3 1.9 convolution_convert_fusion.5
  388.2 0.0 all-reduce.4.cloned.1.call-update
  388.2 44.4 %all-reduce.4.cloned.1.call-done = (bf16[512,768]{1,0:T(8,128)(2,1)}, bf16[512,768]{1,0:T(8,128)(2,1)}) async-done(((bf16[512,768]{1,0:T(8,128)(2,1)}, bf16[512,768]{1,0:T(8,128)(2,1)}), (bf16[512,768]{1,0:T(8,128)(2,1)}, bf16[512,768]{1,0:T(8,128)(2,1)})) %all-reduce.4.cloned.1.call-update) | async-done | bytes 1572880 | tf_op jit(solution)/shard_map/psum | solution.py:90
  432.6 2.2 convolution_convert_fusion.3
  434.7 1.1 copy.75
  435.8 6.8 %all-to-all-start.4 = ((bf16[2,16,16,1024]{3,2,0,1:T(8,128)(2,1)}), bf16[2,16,16,1024]{3,2,0,1:T(8,128)(2,1)}, u32[]{:S(2)}, u32[]{:S(2)}) async-start(bf16[2,16,16,1024]{3,2,0,1:T(8,128)(2,1)} %copy.75), calls=%async_computation.4 | async-start | bytes 2097152 | tf_op jit(solution)/shard_map/all_to_all | solution.py:103
  442.7 24.0 %fusion.1 = (f32[16,49152]{1,0:T(8,128)S(1)}, f32[16,49152]{1,0:T(8,128)}) fusion(bf16[16,4,49152]{2,1,0:T(4,128)(2,1)} %all-to-all-done.3), kind=kLoop, calls=%fused_computation.5 | loop fusion | flops 3145728 | bytes 9437184 | tf_op jit(solution)/shard_map/mul | solution.py:125
  466.7 3.3 mul.85
  470.0 2.0 mul.92
  472.0 4.8 fusion.13
  476.8 0.0 copy-done.6
  476.9 2.4 fusion.12
  479.3 0.0 all-to-all-done.4
  479.3 1.3 copy.76
  480.6 4.6 all_to_all.53
  485.2 1.1 copy.77
  486.3 0.3 copy.82
  486.5 1.2 convolution_convert_fusion.2
  (22 shorter events, 0.1 us)
Async XLA Ops:
  7.2 3.9 copy-start
  14.9 51.5 %all-to-all-start = ((bf16[1,2,16,16,2048]{4,3,1,0,2:T(8,128)(2,1)}), bf16[1,2,16,16,2048]{4,3,1,0,2:T(8,128)(2,1)}, u32[]{:S(2)}, u32[]{:S(2)}) async-start(bf16[1,2,16,16,2048]{4,3,1,0,2:T(8,128)(2,1)} %pad_maximum_fusion.1), calls=%async_computation | async-start | bytes 4194304 | tf_op jit(solution)/shard_map/all_to_all | solution.py:75
  62.9 13.7 %copy-start.9 = (s32[16]{0:T(128)S(1)}, s32[16]{0:T(128)}, u32[]{:S(2)}) copy-start(s32[16]{0:T(128)} %param.15) | copy-start | bytes 196
  66.4 126.3 %all-to-all-start.2 = ((bf16[16,4,49152]{2,1,0:T(4,128)(2,1)}), bf16[16,4,49152]{2,1,0:T(4,128)(2,1)}, u32[]{:S(2)}, u32[]{:S(2)}) async-start(bf16[16,4,49152]{2,1,0:T(4,128)(2,1)} %pad_maximum_fusion), calls=%async_computation.2 | async-start | bytes 12582912 | tf_op jit(solution)/shard_map/all_to_all | solution.py:16
  192.8 22.5 %all-to-all-start.1 = ((bf16[2,2,262144]{2,1,0:T(2,128)(2,1)}), bf16[2,2,262144]{2,1,0:T(2,128)(2,1)S(1)}, u32[]{:S(2)}, u32[]{:S(2)}) async-start(bf16[2,2,262144]{2,1,0:T(2,128)(2,1)} %reshape.97), calls=%async_computation.1 | async-start | bytes 4194304 | tf_op jit(solution)/shard_map/all_to_all | solution.py:74
  215.2 148.9 %all-to-all-start.3 = ((bf16[16,4,49152]{2,1,0:T(4,128)(2,1)}), bf16[16,4,49152]{2,1,0:T(4,128)(2,1)}, u32[]{:S(2)}, u32[]{:S(2)}) async-start(bf16[16,4,49152]{2,1,0:T(4,128)(2,1)} %broadcast_select_fusion), calls=%async_computation.3 | async-start | bytes 12582912 | tf_op jit(solution)/shard_map/all_to_all | solution.py:18
  243.9 188.7 %all-reduce.4.cloned.1.call-start = ((), (), s32[]{:S(2)}) async-start(), calls=%async_computation.6 | async-start | bytes 3145728 | tf_op jit(solution)/shard_map/psum | solution.py:90
  381.2 1.8 copy-start.3
  383.0 3.3 copy-start.4
  383.0 3.3 copy-start.5
  435.8 43.4 %all-to-all-start.4 = ((bf16[2,16,16,1024]{3,2,0,1:T(8,128)(2,1)}), bf16[2,16,16,1024]{3,2,0,1:T(8,128)(2,1)}, u32[]{:S(2)}, u32[]{:S(2)}) async-start(bf16[2,16,16,1024]{3,2,0,1:T(8,128)(2,1)} %copy.75), calls=%async_computation.4 | async-start | bytes 2097152 | tf_op jit(solution)/shard_map/all_to_all | solution.py:103
  472.0 4.8 copy-start.2
  472.0 4.8 copy-start.6
  472.0 4.8 copy-start.7
  472.0 4.8 copy-start.8
  485.2 2.5 copy-start.1
Sparse Core Ops, SparseCore 0:
  388.3 44.2 all-reduce.3
where the time goes:
time: 501 us; the launch traced here: 495 us
  waiting for transfers between devices  195 us (39%)
  local copies, waits for them, and re-layouts  151 us (30%)
  starting transfers between devices  58.5 us (12%)
  other arithmetic  52.7 us (11%)
  matrix products  18.1 us (4%)
  between operations  14.5 us (3%)
    all_to_all x1, waiting for transfers between devices, swap_slots(): lax.all_to_all(picked, 'expert', split_axis=0, concat_axis=0, tiled=True)  80.4 us
    all_to_all x1, waiting for transfers between devices, swap_slots(): lax.all_to_all(stacked, 'expert', split_axis=0, concat_axis=0, tiled=True)  66.7 us
    unnamed x25, local copies, waits for them, and re-layouts  45.6 us
    psum x1, waiting for transfers between devices, body(): lax.psum(pre_part.astype(jnp.bfloat16), 'dp').astype(jnp.float32)  44.4 us
    all_to_all x1, starting transfers between devices, swap_slots(): lax.all_to_all(picked, 'expert', split_axis=0, concat_axis=0, tiled=True)  28.6 us
    mul x1, other arithmetic, body(): MOMENT_DECAY * down_moment.astype(jnp.float32)  24 us
    all_to_all x1, local copies, waits for them, and re-layouts, body(): lax.all_to_all(outgoing, 'expert', split_axis=2, concat_axis=2, tiled=True)  23.4 us
    another operation x4, local copies, waits for them, and re-layouts, swap_slots(): jnp.stack([array_item.reshape(slot_count, -1) for array_item in arrays],...  22.6 us
  transfers between devices with their start and end apart: 6, of which 4 were waited for; matrix products, arithmetic and copies ran while one was open for 37% of the time, Pallas kernels for 0%

commit v1 on v0

--- a/solution.py
+++ b/solution.py
@@ -127,9 +127,104 @@
     return (layer_out, new_up, new_down)
 
 
+def own_weights(expert_ids, route_weight, holder, slot_count):
+    slot_range = jnp.arange(slot_count, dtype=jnp.int32)
+    ids_hit = expert_ids[:, :, None] == slot_range[None, None, :]
+    by_expert = jnp.sum(jnp.where(ids_hit, route_weight[:, :, None], 0.0), axis=1)
+    placed = holder[:, None] == slot_range[None, :]
+    by_slot = jnp.sum(jnp.where(placed[None], by_expert[:, :, None], 0.0), axis=1)
+    return by_slot
+
+
+def move_slots(array_item, partner, slot_count):
+    rows, columns = array_item.shape
+    pieces = array_item.reshape(slot_count, rows // slot_count, columns)
+    spread = lax.all_to_all(pieces, "expert", split_axis=0, concat_axis=0, tiled=True)
+    picked = jnp.take(spread, partner, axis=0)
+    landed = lax.all_to_all(picked, "expert", split_axis=0, concat_axis=0, tiled=True)
+    return landed.reshape(1, rows, columns)
+
+
+def dense_body(
+    tokens,
+    expert_ids,
+    route_weight,
+    cotangent,
+    holder,
+    partner,
+    up_weight,
+    down_weight,
+    up_moment,
+    down_moment,
+):
+    n_slots = lax.axis_size("expert")
+    tok_count, feature_count = tokens.shape
+    half = feature_count // 2
+    swap_pair = [(0, 1), (1, 0)]
+    me = lax.axis_index("expert")
+    by_slot = own_weights(expert_ids, route_weight, holder, n_slots)
+    gathered_weights = lax.all_gather(by_slot, ("expert", "dp"), axis=0, tiled=True)
+    scale = jnp.sum(
+        jnp.where(jnp.arange(n_slots)[None, :] == me, gathered_weights, 0.0), axis=1, keepdims=True
+    )
+    both = lax.all_to_all(
+        jnp.stack([tokens, cotangent]), "dp", split_axis=2, concat_axis=1, tiled=True
+    )
+    every = lax.all_gather(both, "expert", axis=1, tiled=True)
+    rows, cots = every[0], every[1]
+    grads = (scale * cots.astype(jnp.float32)).astype(jnp.bfloat16)
+    up_local, down_local = up_weight[0], down_weight[0]
+    pre_part = jnp.dot(rows, up_local, preferred_element_type=jnp.float32).astype(jnp.bfloat16)
+    back_part = lax.dot_general(
+        grads, down_local, (((1,), (1,)), ((), ())), preferred_element_type=jnp.float32
+    ).astype(jnp.bfloat16)
+    preact = pre_part.astype(jnp.float32) + lax.ppermute(pre_part, "dp", swap_pair).astype(
+        jnp.float32
+    )
+    back_sum = back_part.astype(jnp.float32) + lax.ppermute(back_part, "dp", swap_pair).astype(
+        jnp.float32
+    )
+    hidden = jax.nn.silu(preact).astype(jnp.bfloat16)
+    pre_grad = (back_sum * silu_slope(preact)).astype(jnp.bfloat16)
+    up_grad = lax.dot_general(
+        rows, pre_grad, (((0,), (0,)), ((), ())), preferred_element_type=jnp.float32
+    )
+    new_up = (
+        MOMENT_DECAY * up_moment[0].astype(jnp.float32) + (1.0 - MOMENT_DECAY) * up_grad
+    ).astype(jnp.bfloat16)
+    down_grad = lax.dot_general(
+        hidden, grads, (((0,), (0,)), ((), ())), preferred_element_type=jnp.float32
+    )
+    new_down = (
+        MOMENT_DECAY * down_moment[0].astype(jnp.float32) + (1.0 - MOMENT_DECAY) * down_grad
+    ).astype(jnp.bfloat16)
+    out_part = jnp.dot(hidden, down_local, preferred_element_type=jnp.float32).astype(jnp.bfloat16)
+    out_part = (scale * out_part.astype(jnp.float32)).astype(jnp.bfloat16)
+    moved_up = move_slots(new_up, partner, n_slots)
+    moved_down = move_slots(new_down, partner, n_slots)
+    parts = lax.all_to_all(
+        out_part.reshape(n_slots, 2 * tok_count, half),
+        "expert",
+        split_axis=0,
+        concat_axis=0,
+        tiled=True,
+    )
+    summed = jnp.sum(parts.astype(jnp.float32), axis=0).astype(jnp.bfloat16)
+    layer_out = lax.all_to_all(summed, "dp", split_axis=0, concat_axis=1, tiled=True)
+    return (layer_out, moved_up, moved_down)
+
+
+def pick_body(mesh):
+    def chosen(tokens, *others):
+        dense = mesh.shape["dp"] == 2 and tokens.shape[0] * mesh.size <= 2048
+        return (dense_body if dense else body)(tokens, *others)
+
+    return chosen
+
+
 def solution(mesh):
     return jax.shard_map(
-        body,
+        pick_body(mesh),
         mesh=mesh,
         in_specs=(
             P(("expert", "dp"), None),

time: 501 us -> 324 us (0.65)
  local copies, waits for them, and re-layouts: 151 us -> 17.6 us
  blocking collectives: 4.58 us -> 52 us
  other arithmetic: 52.7 us -> 7.21 us
  starting transfers between devices: 58.5 us -> 35.8 us
  waiting for transfers between devices: 195 us -> 176 us
    psum x1 -> x0, waiting for transfers between devices: 44.4 us -> none  [body(): lax.psum(pre_part.astype(jnp.bfloat16), 'dp').astype(jnp.float32)]
    all_gather x0 -> x1, blocking collectives: none -> 44.2 us  [dense_body(): lax.all_gather(by_slot, ('expert', 'dp'), axis=0, tiled=True)]
    all_to_all x4 -> x2, local copies, waits for them, and re-layouts: 43.3 us -> 2.39 us  [the longest x1 1.74 us: dense_body(): lax.all_to_all(jnp.stack([tokens, cotangent]), 'dp', split_axis=2, concat...]
    unnamed x25, local copies, waits for them, and re-layouts: 45.6 us -> 7.99 us
    all_gather x0 -> x1, waiting for transfers between devices: none -> 26.7 us  [dense_body(): every = lax.all_gather(both, 'expert', axis=1, tiled=True)]
    another operation x7 -> x1, local copies, waits for them, and re-layouts: 25.9 us -> 0.74 us  [dense_body(): jnp.stack([tokens, cotangent])]
    mul x1 -> x0, other arithmetic: 24 us -> none  [body(): MOMENT_DECAY * down_moment.astype(jnp.float32)]
    all_to_all x5, starting transfers between devices: 58 us -> 35.2 us  [the longest x2 15.3 us: move_slots(): lax.all_to_all(picked, 'expert', split_axis=0, concat_axis=0, tiled=True)]
  transfers between devices with their start and end apart: 6 -> 8, of which waited for: 4 -> 8; matrix products, arithmetic and copies ran while one was open for 37% -> 8% of each run, Pallas kernels for 0% -> 0%
where the time goes in v1:
time: 324 us; the launch traced here: 321 us
  waiting for transfers between devices  176 us (54%)
  blocking collectives  52 us (16%)
  starting transfers between devices  35.8 us (11%)
  matrix products  18.1 us (6%)
  local copies, waits for them, and re-layouts  17.6 us (5%)
  between operations  14.3 us (4%)
  other arithmetic  7.21 us (2%)
    all_to_all x2, waiting for transfers between devices, move_slots(): lax.all_to_all(picked, 'expert', split_axis=0, concat_axis=0, tiled=True)  61.2 us
    all_to_all x2, waiting for transfers between devices, move_slots(): lax.all_to_all(pieces, 'expert', split_axis=0, concat_axis=0, tiled=True)  57.3 us
    all_gather x1, blocking collectives, dense_body(): lax.all_gather(by_slot, ('expert', 'dp'), axis=0, tiled=True)  44.2 us
    all_to_all x1, waiting for transfers between devices, dense_body(): lax.all_to_all(out_part.reshape(n_slots, 2 * tok_count, half), 'expert',...  28.2 us
    all_gather x1, waiting for transfers between devices, dense_body(): every = lax.all_gather(both, 'expert', axis=1, tiled=True)  26.7 us
    all_to_all x2, starting transfers between devices, move_slots(): lax.all_to_all(picked, 'expert', split_axis=0, concat_axis=0, tiled=True)  15.3 us
    all_to_all x2, starting transfers between devices, move_slots(): lax.all_to_all(pieces, 'expert', split_axis=0, concat_axis=0, tiled=True)  11.6 us
    all_to_all x1, starting transfers between devices, dense_body(): lax.all_to_all(out_part.reshape(n_slots, 2 * tok_count, half), 'expert',...  8.25 us
  transfers between devices with their start and end apart: 8, of which 8 were waited for; matrix products, arithmetic and copies ran while one was open for 8% of the time, Pallas kernels for 0%

profile of v1, /device:TPU:0, one launch (start us, length us, event | category | flops | bytes accessed | tf_op | source)
XLA Modules:
  0.0 321.0 jit_solution(17718335361258816803)
XLA Ops:
  7.2 0.0 copy-start
  7.2 0.0 all-gather.3.cloned.1.call-start
  7.2 1.1 pad_maximum_fusion
  8.3 0.7 copy.36
  9.0 1.4 reshape.95
  10.4 0.0 copy-start.2
  10.4 0.0 copy-start.3
  10.4 0.0 copy-start.4
  10.4 4.0 %all_to_all.62 = bf16[2,2,24576]{2,1,0:T(2,128)(2,1)S(1)} all-to-all(bf16[2,2,24576]{2,1,0:T(2,128)(2,1)S(1)} %reshape.95), channel_id=1, replica_groups=mesh['expert'=16,'dp'=2] {'dp'}, dimensions={0} | all-to-all | bytes 393216 | tf_op jit(solution)/shard_map/all_to_all | solution.py:170
  14.5 1.5 reshape.96
  15.9 1.7 copy.37
  17.7 0.0 all-gather.3.cloned.1.call-update
  17.7 0.0 copy-done.2
  17.7 0.0 copy-done.3
  17.8 0.0 copy-done.4
  17.8 0.1 iota_compare_fusion.1
  17.8 0.1 select_reduce_fusion
  18.0 44.2 %all-gather = f32[32,24,16]{1,2,0:T(8,128)S(1)} all-gather(f32[1,24,16]{1,2,0:T(8,128)S(1)} %bitcast.70), channel_id=1, replica_groups=mesh['expert'=16,'dp'=2] {'expert','dp'}, dimensions={0}, use_global_device_ids=true | all-gather | bytes 50688 | tf_op jit(solution)/shard_map/all_gather | solution.py:166
  62.2 0.1 copy.35
  62.3 0.2 reshape.94
  62.5 0.1 select_reduce_fusion.2
  62.5 26.7 %all-gather.3.cloned.1.call-done = bf16[2,768,1024]{2,1,0:T(8,128)(2,1)} async-done(((bf16[2,48,1024]{2,1,0:T(8,128)(2,1)}), bf16[2,768,1024]{2,1,0:T(8,128)(2,1)}) %all-gather.3.cloned.1.call-update) | async-done | bytes 3145744 | tf_op jit(solution)/shard_map/all_gather | solution.py:173
  89.3 0.0 copy-start.5
  89.3 3.4 %fusion.15 = bf16[768,768]{1,0:T(8,128)(2,1)S(1)} fusion(bf16[1,1024,768]{2,1,0:T(8,128)(2,1)} %param.16, bf16[2,768,1024]{2,1,0:T(8,128)(2,1)} %all-gather.3.cloned.1.call-done), kind=kOutput, calls=%fused_computation.28 | convolution fusion | flops 1208549376 | bytes 4325376 | tf_op jit(solution)/shard_map/dot_general | solution.py:177
  92.7 0.0 copy-start.7
  92.7 0.0 copy-start.6
  92.7 0.1 collective-permute-start
  92.8 0.0 copy-done
  92.8 0.0 copy-done.5
  92.8 1.4 fusion.18
  94.3 0.6 collective-permute-start.1
  94.8 0.8 collective-permute-done
  95.6 0.0 copy-start.8
  95.6 1.7 collective-permute-done.1
  97.3 0.0 copy-done.7
  97.3 0.0 copy-done.6
  97.3 3.4 %fusion.4 = bf16[1024,768]{1,0:T(8,128)(2,1)} fusion(bf16[1,1024,768]{2,1,0:T(8,128)(2,1)S(1)} %copy-done.6, bf16[2,768,1024]{2,1,0:T(8,128)(2,1)S(1)} %copy-done.5, bf16[768,768]{1,0:T(8,128)(2,1)S(1)} %collective-permute-done.1, bf16[768,768]{1,0:T(8,128)(2,1)S(1)} %fusion.18, bf16[768,768]{1,0:T(8,128)(2,1)S(1)} %collective-permute-done, ...), kind=kOutput, calls=%fused_computation.10 | convolution fusion | flops 1220739072 | bytes 9437184 | tf_op jit(solution)/shard_map/dot_general | solution.py:189
  100.7 0.0 copy-done.8
  100.7 4.1 %all-to-all-start.3 = ((bf16[16,64,768]{2,1,0:T(8,128)(2,1)}), bf16[16,64,768]{2,1,0:T(8,128)(2,1)S(1)}, u32[]{:S(2)}, u32[]{:S(2)}) async-start(bf16[16,64,768]{2,1,0:T(8,128)(2,1)} %bitcast.63), calls=%async_computation.3 | async-start | bytes 3145728 | tf_op jit(solution)/shard_map/all_to_all | solution.py:142
  104.8 4.3 %multiply_convert_fusion = bf16[768,1024]{1,0:T(8,128)(2,1)} fusion(f32[768]{0:T(1024)S(1)} %select_reduce_fusion.2, bf16[1,768,1024]{2,1,0:T(8,128)(2,1)S(1)} %copy-done, bf16[768,768]{1,0:T(8,128)(2,1)} %copy-done.8, bf16[768,768]{1,0:T(8,128)(2,1)} %copy-done.7), kind=kOutput, calls=%fused_computation.11 | convolution fusion | flops 1215823872 | bytes 5508096 | tf_op jit(solution)/shard_map/dot_general | solution.py:201
  109.1 30.0 %all-to-all-done.3 = bf16[16,64,768]{2,1,0:T(8,128)(2,1)S(1)} async-done(((bf16[16,64,768]{2,1,0:T(8,128)(2,1)}), bf16[16,64,768]{2,1,0:T(8,128)(2,1)S(1)}, u32[]{:S(2)}, u32[]{:S(2)}) %all-to-all-start.3) | async-done | bytes 1572896 | tf_op jit(solution)/shard_map/all_to_all | solution.py:142
  139.0 0.0 copy-start.1
  139.0 1.1 copy-done.1
  140.2 8.2 %all-to-all-start.1 = ((bf16[16,48,1024]{2,1,0:T(8,128)(2,1)}), bf16[16,48,1024]{2,1,0:T(8,128)(2,1)S(1)}, u32[]{:S(2)}, u32[]{:S(2)}) async-start(bf16[16,48,1024]{2,1,0:T(8,128)(2,1)} %bitcast.62), calls=%async_computation.1 | async-start | bytes 3145728 | tf_op jit(solution)/shard_map/all_to_all | solution.py:205
  148.4 5.6 %fusion.3 = bf16[768,1024]{1,0:T(8,128)(2,1)} fusion(bf16[1,768,1024]{2,1,0:T(8,128)(2,1)} %param.19, f32[768]{0:T(1024)S(1)} %select_reduce_fusion.2, bf16[2,768,1024]{2,1,0:T(8,128)(2,1)} %all-gather.3.cloned.1.call-done, bf16[768,768]{1,0:T(8,128)(2,1)} %copy-done.8, bf16[768,768]{1,0:T(8,128)(2,1)} %copy-done.7), kind=kOutput, calls=%fused_computation.8 | convolution fusion | flops 1218969600 | bytes 7080960 | tf_op jit(solution)/shard_map/dot_general | solution.py:195
  154.1 28.2 %all-to-all-done.1 = bf16[16,48,1024]{2,1,0:T(8,128)(2,1)S(1)} async-done(((bf16[16,48,1024]{2,1,0:T(8,128)(2,1)}), bf16[16,48,1024]{2,1,0:T(8,128)(2,1)S(1)}, u32[]{:S(2)}, u32[]{:S(2)}) %all-to-all-start.1) | async-done | bytes 1572896 | tf_op jit(solution)/shard_map/all_to_all | solution.py:205
  182.2 0.0 copy-start.9
  182.2 7.5 %all-to-all-start.5 = ((bf16[16,48,1024]{2,1,0:T(8,128)(2,1)}), bf16[16,48,1024]{2,1,0:T(8,128)(2,1)}, u32[]{:S(2)}, u32[]{:S(2)}) async-start(bf16[16,48,1024]{2,1,0:T(8,128)(2,1)} %bitcast.61), calls=%async_computation.5 | async-start | bytes 3145728 | tf_op jit(solution)/shard_map/all_to_all | solution.py:142
  189.7 0.0 copy-done.9
  189.8 3.2 gather_fusion
  193.0 0.3 reduce_sum.42
  193.3 2.8 broadcast_select_fusion.1
  196.0 27.3 %all-to-all-done.5 = bf16[16,48,1024]{2,1,0:T(8,128)(2,1)} async-done(((bf16[16,48,1024]{2,1,0:T(8,128)(2,1)}), bf16[16,48,1024]{2,1,0:T(8,128)(2,1)}, u32[]{:S(2)}, u32[]{:S(2)}) %all-to-all-start.5) | async-done | bytes 1572896 | tf_op jit(solution)/shard_map/all_to_all | solution.py:142
  223.4 3.8 %all_to_all.63 = bf16[2,24,1024]{2,1,0:T(8,128)(2,1)S(1)} all-to-all(bf16[2,24,1024]{2,1,0:T(8,128)(2,1)S(1)} %bitcast.66), channel_id=1, replica_groups=mesh['expert'=16,'dp'=2] {'dp'}, dimensions={0} | all-to-all | bytes 196608 | tf_op jit(solution)/shard_map/all_to_all | solution.py:213
  227.2 7.3 %all-to-all-start.4 = ((bf16[16,64,768]{2,1,0:T(8,128)(2,1)}), bf16[16,64,768]{2,1,0:T(8,128)(2,1)S(1)}, u32[]{:S(2)}, u32[]{:S(2)}) async-start(bf16[16,64,768]{2,1,0:T(8,128)(2,1)} %broadcast_select_fusion.1), calls=%async_computation.4 | async-start | bytes 3145728 | tf_op jit(solution)/shard_map/all_to_all | solution.py:144
  234.4 3.2 gather_fusion.1
  237.6 2.8 broadcast_select_fusion
  240.4 28.3 %all-to-all-done.4 = bf16[16,64,768]{2,1,0:T(8,128)(2,1)S(1)} async-done(((bf16[16,64,768]{2,1,0:T(8,128)(2,1)}), bf16[16,64,768]{2,1,0:T(8,128)(2,1)S(1)}, u32[]{:S(2)}, u32[]{:S(2)}) %all-to-all-start.4) | async-done | bytes 1572896 | tf_op jit(solution)/shard_map/all_to_all | solution.py:144
  268.7 8.1 %all-to-all-start.6 = ((bf16[16,48,1024]{2,1,0:T(8,128)(2,1)}), bf16[16,48,1024]{2,1,0:T(8,128)(2,1)}, u32[]{:S(2)}, u32[]{:S(2)}) async-start(bf16[16,48,1024]{2,1,0:T(8,128)(2,1)} %broadcast_select_fusion), calls=%async_computation.6 | async-start | bytes 3145728 | tf_op jit(solution)/shard_map/all_to_all | solution.py:144
  276.8 0.6 copy.39
  277.4 32.9 %all-to-all-done.6 = bf16[16,48,1024]{2,1,0:T(8,128)(2,1)} async-done(((bf16[16,48,1024]{2,1,0:T(8,128)(2,1)}), bf16[16,48,1024]{2,1,0:T(8,128)(2,1)}, u32[]{:S(2)}, u32[]{:S(2)}) %all-to-all-start.6) | async-done | bytes 1572896 | tf_op jit(solution)/shard_map/all_to_all | solution.py:144
  310.3 1.1 copy.42
  311.5 2.7 copy.43
  (5 shorter events, 0.0 us)
Async XLA Ops:
  7.2 85.6 %copy-start = (bf16[1,768,1024]{2,1,0:T(8,128)(2,1)S(1)}, bf16[1,768,1024]{2,1,0:T(8,128)(2,1)}, u32[]{:S(2)}) copy-start(bf16[1,768,1024]{2,1,0:T(8,128)(2,1)} %param.17) | copy-start | bytes 4718596
  7.2 82.1 %all-gather.3.cloned.1.call-start = ((), (), s32[]{:S(2)}) async-start(), calls=%async_computation.7 | async-start | bytes 3342336 | tf_op jit(solution)/shard_map/all_gather | solution.py:173
  10.4 7.3 %copy-start.2 = (f32[24,8]{0,1:T(8,128)S(1)}, f32[24,8]{0,1:T(8,128)}, u32[]{:S(2)}) copy-start(f32[24,8]{0,1:T(8,128)} %param.12) | copy-start | bytes 2308
  10.4 7.3 %copy-start.3 = (s32[24,8]{0,1:T(8,128)S(1)}, s32[24,8]{0,1:T(8,128)}, u32[]{:S(2)}) copy-start(s32[24,8]{0,1:T(8,128)} %param.11) | copy-start | bytes 2308
  10.4 7.3 %copy-start.4 = (s32[16]{0:T(128)S(1)}, s32[16]{0:T(128)}, u32[]{:S(2)}) copy-start(s32[16]{0:T(128)} %param.14) | copy-start | bytes 196
  89.3 3.5 %copy-start.5 = (bf16[2,768,1024]{2,1,0:T(8,128)(2,1)S(1)}, bf16[2,768,1024]{2,1,0:T(8,128)(2,1)}, u32[]{:S(2)}) copy-start(bf16[2,768,1024]{2,1,0:T(8,128)(2,1)} %all-gather.3.cloned.1.call-done) | copy-start | bytes 9437188
  92.7 4.6 %copy-start.7 = (bf16[768,768]{1,0:T(8,128)(2,1)}, bf16[768,768]{1,0:T(8,128)(2,1)S(1)}, u32[]{:S(2)}) copy-start(bf16[768,768]{1,0:T(8,128)(2,1)S(1)} %fusion.15) | copy-start | bytes 3538948
  92.7 4.6 %copy-start.6 = (bf16[1,1024,768]{2,1,0:T(8,128)(2,1)S(1)}, bf16[1,1024,768]{2,1,0:T(8,128)(2,1)}, u32[]{:S(2)}) copy-start(bf16[1,1024,768]{2,1,0:T(8,128)(2,1)} %param.18) | copy-start | bytes 4718596
  92.7 2.9 collective-permute-start
  94.3 3.0 collective-permute-start.1
  95.6 5.0 %copy-start.8 = (bf16[768,768]{1,0:T(8,128)(2,1)}, bf16[768,768]{1,0:T(8,128)(2,1)S(1)}, u32[]{:S(2)}) copy-start(bf16[768,768]{1,0:T(8,128)(2,1)S(1)} %collective-permute-done) | copy-start | bytes 3538948
  100.7 38.4 %all-to-all-start.3 = ((bf16[16,64,768]{2,1,0:T(8,128)(2,1)}), bf16[16,64,768]{2,1,0:T(8,128)(2,1)S(1)}, u32[]{:S(2)}, u32[]{:S(2)}) async-start(bf16[16,64,768]{2,1,0:T(8,128)(2,1)} %bitcast.63), calls=%async_computation.3 | async-start | bytes 3145728 | tf_op jit(solution)/shard_map/all_to_all | solution.py:142
  139.0 1.1 copy-start.1
  140.2 42.0 %all-to-all-start.1 = ((bf16[16,48,1024]{2,1,0:T(8,128)(2,1)}), bf16[16,48,1024]{2,1,0:T(8,128)(2,1)S(1)}, u32[]{:S(2)}, u32[]{:S(2)}) async-start(bf16[16,48,1024]{2,1,0:T(8,128)(2,1)} %bitcast.62), calls=%async_computation.1 | async-start | bytes 3145728 | tf_op jit(solution)/shard_map/all_to_all | solution.py:205
  182.2 7.5 %copy-start.9 = (s32[16]{0:T(128)S(1)}, s32[16]{0:T(128)}, u32[]{:S(2)}) copy-start(s32[16]{0:T(128)} %param.15) | copy-start | bytes 196
  182.2 41.2 %all-to-all-start.5 = ((bf16[16,48,1024]{2,1,0:T(8,128)(2,1)}), bf16[16,48,1024]{2,1,0:T(8,128)(2,1)}, u32[]{:S(2)}, u32[]{:S(2)}) async-start(bf16[16,48,1024]{2,1,0:T(8,128)(2,1)} %bitcast.61), calls=%async_computation.5 | async-start | bytes 3145728 | tf_op jit(solution)/shard_map/all_to_all | solution.py:142
  227.2 41.5 %all-to-all-start.4 = ((bf16[16,64,768]{2,1,0:T(8,128)(2,1)}), bf16[16,64,768]{2,1,0:T(8,128)(2,1)S(1)}, u32[]{:S(2)}, u32[]{:S(2)}) async-start(bf16[16,64,768]{2,1,0:T(8,128)(2,1)} %broadcast_select_fusion.1), calls=%async_computation.4 | async-start | bytes 3145728 | tf_op jit(solution)/shard_map/all_to_all | solution.py:144
  268.7 41.6 %all-to-all-start.6 = ((bf16[16,48,1024]{2,1,0:T(8,128)(2,1)}), bf16[16,48,1024]{2,1,0:T(8,128)(2,1)}, u32[]{:S(2)}, u32[]{:S(2)}) async-start(bf16[16,48,1024]{2,1,0:T(8,128)(2,1)} %broadcast_select_fusion), calls=%async_computation.6 | async-start | bytes 3145728 | tf_op jit(solution)/shard_map/all_to_all | solution.py:144
Sparse Core Ops, SparseCore 0:
  17.8 71.3 all-gather.2

commit v2 on v1

--- a/solution.py
+++ b/solution.py
@@ -1,6 +1,8 @@
 import jax
 import jax.numpy as jnp
 from jax import lax
+from jax.experimental import pallas as pl
+from jax.experimental.pallas import tpu as pltpu
 from jax.sharding import PartitionSpec as P
 
 MOMENT_DECAY = 0.9
@@ -136,13 +138,322 @@
     return by_slot
 
 
-def move_slots(array_item, partner, slot_count):
-    rows, columns = array_item.shape
-    pieces = array_item.reshape(slot_count, rows // slot_count, columns)
-    spread = lax.all_to_all(pieces, "expert", split_axis=0, concat_axis=0, tiled=True)
-    picked = jnp.take(spread, partner, axis=0)
-    landed = lax.all_to_all(picked, "expert", split_axis=0, concat_axis=0, tiled=True)
-    return landed.reshape(1, rows, columns)
+MESH = pl.DeviceIdType.MESH
+CHUNKS = 4
+
+
+def route_table(partner, me):
+    slots = jnp.arange(16, dtype=jnp.int32)
+    z, half = me // 4, me // 8
+    pair_plane = lax.bitwise_xor(z, 1)
+    inner = (z == 1) | (z == 2)
+    crosses = (partner // 8) != (slots // 8)
+    count = jnp.cumsum(crosses.reshape(2, 8).astype(jnp.int32), axis=1).reshape(16) - 1
+    rank = jnp.clip(count, 0, 3)
+    quad = jnp.arange(4, dtype=jnp.int32)
+    leaving = crosses & (slots // 8 != half)
+    hit = leaving[None, :] & (count[None, :] == quad[:, None])
+    source = jnp.sum(jnp.where(hit, partner[None, :], 0), axis=1)
+    cross_kind = jnp.where(source // 4 == z, 0, 1)
+    cross_at = source % 4
+
+    def pick(array_item, start):
+        return lax.dynamic_slice(array_item, (start,), (4,))
+
+    pass_source, pass_rank = pick(partner, pair_plane * 4), pick(rank, pair_plane * 4)
+    pass_kind = jnp.where(pass_source // 4 == z, 0, 2)
+    pass_at = jnp.where(pass_kind == 0, pass_source % 4, pass_rank)
+    end_source, end_rank = pick(partner, z * 4), pick(rank, z * 4)
+    end_plane = end_source // 4
+    inner_kind = jnp.where(end_plane == z, 0, jnp.where(end_plane == pair_plane, 1, 2))
+    inner_at = jnp.where(inner_kind == 2, end_rank, end_source % 4)
+    outer_kind = jnp.where(end_plane == z, 0, 1)
+    outer_at = jnp.where(outer_kind == 0, end_source % 4, quad)
+    end_kind = jnp.where(inner, inner_kind, outer_kind)
+    end_at = jnp.where(inner, inner_at, outer_at)
+    return jnp.concatenate([cross_kind, cross_at, pass_kind, pass_at, end_kind, end_at]).astype(
+        jnp.int32
+    )
+
+
+def swap_kernel(*refs):
+    table, new_up, new_down, outs, up_end, down_end, layer = refs[:7]
+    scratch = list(refs[7:])
+    total = 2 * CHUNKS
+
+    def take(number):
+        taken = scratch[:number]
+        del scratch[:number]
+        return taken
+
+    own, pair, cross, landed, passed, final = [take(total) for _ in range(6)]
+    plane_in, plane_sum, line_in, core_sum, core_in = take(5)
+    (
+        spread_send,
+        spread_recv,
+        pair_send,
+        pair_recv,
+        cross_send,
+        cross_recv,
+        end_send,
+        end_recv,
+        plane_send,
+        plane_recv,
+        line_send,
+        line_recv,
+        core_send,
+        core_recv,
+    ) = scratch
+    me = lax.axis_index("expert")
+    core = lax.axis_index("dp")
+    z, spot = me // 4, me % 4
+    inner = (z == 1) | (z == 2)
+    plane_peers = [z * 4 + lax.bitwise_xor(spot, r) for r in (1, 2, 3)]
+    line_peers = [lax.bitwise_xor(z, r) * 4 + spot for r in (1, 2, 3)]
+    pair_peer, cross_peer = line_peers[0], line_peers[2]
+
+    barrier = pltpu.get_barrier_semaphore()
+    for peer in plane_peers + line_peers:
+        pl.semaphore_signal(barrier, inc=1, device_id=(peer, core), device_id_type=MESH)
+    pl.semaphore_signal(barrier, inc=1, device_id=(me, 1 - core), device_id_type=MESH)
+    pl.semaphore_wait(barrier, 7)
+
+    sources = [new_up] * CHUNKS + [new_down] * CHUNKS
+    ends = [up_end] * CHUNKS + [down_end] * CHUNKS
+
+    def remote(src, dst, send, recv, peer, at_core=None):
+        return pltpu.make_async_remote_copy(
+            src_ref=src,
+            dst_ref=dst,
+            send_sem=send,
+            recv_sem=recv,
+            device_id=(peer, core if at_core is None else at_core),
+            device_id_type=MESH,
+        )
+
+    def spread(k, r):
+        return remote(
+            sources[k].at[lax.bitwise_xor(spot, r), k % CHUNKS],
+            own[k].at[spot],
+            spread_send.at[k, r - 1],
+            spread_recv.at[k, r - 1],
+            plane_peers[r - 1],
+        )
+
+    def finish(k, r):
+        return remote(
+            final[k].at[lax.bitwise_xor(spot, r)],
+            ends[k].at[spot, k % CHUNKS],
+            end_send.at[k, r - 1],
+            end_recv.at[k, r - 1],
+            plane_peers[r - 1],
+        )
+
+    def to_pair(k, buffer):
+        return remote(buffer, pair[k], pair_send.at[k], pair_recv.at[k], pair_peer)
+
+    def to_cross(k):
+        return remote(cross[k], landed[k], cross_send.at[k], cross_recv.at[k], cross_peer)
+
+    def plane_copy(r):
+        return remote(
+            outs.at[lax.bitwise_xor(spot, r)],
+            plane_in.at[r - 1],
+            plane_send.at[r - 1],
+            plane_recv.at[r - 1],
+            plane_peers[r - 1],
+        )
+
+    def line_copy(r):
+        return remote(
+            plane_sum.at[lax.bitwise_xor(z, r)],
+            line_in.at[r - 1],
+            line_send.at[r - 1],
+            line_recv.at[r - 1],
+            line_peers[r - 1],
+        )
+
+    def core_copy():
+        return remote(
+            core_sum.at[1 - core], core_in, core_send.at[0], core_recv.at[0], me, 1 - core
+        )
+
+    def fill(target, row, pools):
+        @pl.loop(0, 4)
+        def _(q):
+            kind, at = table[row * 8 + q], table[row * 8 + 4 + q]
+            value = pools[0][1][at].astype(jnp.float32)
+            for code, pool in pools[1:]:
+                value = jnp.where(kind == code, pool[at].astype(jnp.float32), value)
+            target[q] = value.astype(target.dtype)
+
+    def begin(k):
+        for r in (1, 2, 3):
+            spread(k, r).start()
+        own[k][spot] = sources[k][spot, k % CHUNKS]
+
+    def stage_first(k):
+        for r in (1, 2, 3):
+            spread(k, r).wait_recv()
+
+        @pl.when(jnp.logical_not(inner))
+        def _():
+            to_pair(k, own[k]).start()
+
+    def stage_cross(k):
+        @pl.when(inner)
+        def _():
+            to_pair(k, own[k]).wait_recv()
+            fill(cross[k], 0, [(0, own[k]), (1, pair[k])])
+            to_cross(k).start()
+
+    def stage_pass(k):
+        @pl.when(inner)
+        def _():
+            to_cross(k).wait_recv()
+            fill(passed[k], 1, [(0, own[k]), (2, landed[k])])
+            to_pair(k, passed[k]).start()
+            fill(final[k], 2, [(0, own[k]), (1, pair[k]), (2, landed[k])])
+            send_final(k)
+
+    def stage_outer(k):
+        @pl.when(jnp.logical_not(inner))
+        def _():
+            to_pair(k, passed[k]).wait_recv()
+            fill(final[k], 2, [(0, own[k]), (1, pair[k])])
+            send_final(k)
+
+    def send_final(k):
+        for r in (1, 2, 3):
+            finish(k, r).start()
+        ends[k][spot, k % CHUNKS] = final[k][spot]
+
+    for k in range(CHUNKS):
+        begin(k)
+    for r in (1, 2, 3):
+        plane_copy(r).start()
+    for k in range(CHUNKS, total):
+        begin(k)
+
+    for step in range(total + 3):
+        if step < total:
+            stage_first(step)
+        if 0 <= step - 1 < total:
+            stage_cross(step - 1)
+        if 0 <= step - 2 < total:
+            stage_pass(step - 2)
+        if 0 <= step - 3 < total:
+            stage_outer(step - 3)
+        if step == CHUNKS:
+            for r in (1, 2, 3):
+                plane_copy(r).wait_recv()
+
+            @pl.loop(0, 8)
+            def _(n):
+                at, group = n // 2, n % 2
+                value = outs[spot, at, group].astype(jnp.float32)
+                for r in range(3):
+                    value = value + plane_in[r, at, group].astype(jnp.float32)
+                plane_sum[at, group] = value.astype(plane_sum.dtype)
+
+            for r in (1, 2, 3):
+                line_copy(r).start()
+        if step == CHUNKS + 3:
+            for r in (1, 2, 3):
+                line_copy(r).wait_recv()
+            for group in range(2):
+                value = plane_sum[z, group].astype(jnp.float32)
+                for r in range(3):
+                    value = value + line_in[r, group].astype(jnp.float32)
+                core_sum[group] = value.astype(core_sum.dtype)
+            core_copy().start()
+
+    core_copy().wait_recv()
+    half = core_in.shape[1]
+    for group in range(2):
+
+        @pl.when(core == group)
+        def _():
+            layer[:, group * half : (group + 1) * half] = core_sum[group]
+            layer[:, (1 - group) * half : (2 - group) * half] = core_in[...]
+
+    for k in range(total):
+        for r in (1, 2, 3):
+            finish(k, r).wait_recv()
+            finish(k, r).wait_send()
+            spread(k, r).wait_send()
+        to_pair(k, own[k]).wait_send()
+
+        @pl.when(inner)
+        def _():
+            to_cross(k).wait_send()
+
+    for r in (1, 2, 3):
+        plane_copy(r).wait_send()
+        line_copy(r).wait_send()
+    core_copy().wait_send()
+
+
+def swap_and_return(new_up, new_down, outs, partner, me):
+    half, hidden_count = new_up.shape
+    tok_count = outs.shape[0] // 32
+    up_rows, down_rows = half // (4 * CHUNKS), hidden_count // (4 * CHUNKS)
+    up_shape = (4, CHUNKS, up_rows, hidden_count)
+    down_shape = (4, CHUNKS, down_rows, half)
+    kind = new_up.dtype
+    pieces = [pltpu.VMEM((4,) + up_shape[2:], kind)] * CHUNKS + [
+        pltpu.VMEM((4,) + down_shape[2:], kind)
+    ] * CHUNKS
+    total = 2 * CHUNKS
+    dma = pltpu.SemaphoreType.DMA
+    block = (tok_count, half)
+    by_spot = outs.reshape(4, 4, 2, tok_count, half).transpose(1, 0, 2, 3, 4)
+    vmem = pl.BlockSpec(memory_space=pltpu.VMEM)
+    up_end, down_end, layer = pl.pallas_call(
+        swap_kernel,
+        out_shape=(
+            jax.ShapeDtypeStruct(up_shape, kind),
+            jax.ShapeDtypeStruct(down_shape, kind),
+            jax.ShapeDtypeStruct((tok_count, 2 * half), kind),
+        ),
+        in_specs=[pl.BlockSpec(memory_space=pltpu.SMEM), vmem, vmem, vmem],
+        out_specs=(vmem, vmem, vmem),
+        scratch_shapes=pieces * 6
+        + [
+            pltpu.VMEM((3, 4, 2) + block, kind),
+            pltpu.VMEM((4, 2) + block, kind),
+            pltpu.VMEM((3, 2) + block, kind),
+            pltpu.VMEM((2,) + block, kind),
+            pltpu.VMEM(block, kind),
+            dma((total, 3)),
+            dma((total, 3)),
+            dma((total,)),
+            dma((total,)),
+            dma((total,)),
+            dma((total,)),
+            dma((total, 3)),
+            dma((total, 3)),
+            dma((3,)),
+            dma((3,)),
+            dma((3,)),
+            dma((3,)),
+            dma((1,)),
+            dma((1,)),
+        ],
+        compiler_params=pltpu.CompilerParams(
+            collective_id=1, has_side_effects=True, vmem_limit_bytes=56 * 1024 * 1024
+        ),
+    )(
+        route_table(partner, me),
+        new_up.reshape(up_shape),
+        new_down.reshape(down_shape),
+        by_spot,
+    )
+    return (
+        layer,
+        up_end.reshape(1, half, hidden_count),
+        down_end.reshape(1, hidden_count, half),
+    )
 
 
 def dense_body(
@@ -200,23 +511,12 @@
     ).astype(jnp.bfloat16)
     out_part = jnp.dot(hidden, down_local, preferred_element_type=jnp.float32).astype(jnp.bfloat16)
     out_part = (scale * out_part.astype(jnp.float32)).astype(jnp.bfloat16)
-    moved_up = move_slots(new_up, partner, n_slots)
-    moved_down = move_slots(new_down, partner, n_slots)
-    parts = lax.all_to_all(
-        out_part.reshape(n_slots, 2 * tok_count, half),
-        "expert",
-        split_axis=0,
-        concat_axis=0,
-        tiled=True,
-    )
-    summed = jnp.sum(parts.astype(jnp.float32), axis=0).astype(jnp.bfloat16)
-    layer_out = lax.all_to_all(summed, "dp", split_axis=0, concat_axis=1, tiled=True)
-    return (layer_out, moved_up, moved_down)
+    return swap_and_return(new_up, new_down, out_part, partner, me)
 
 
 def pick_body(mesh):
     def chosen(tokens, *others):
-        dense = mesh.shape["dp"] == 2 and tokens.shape[0] * mesh.size <= 2048
+        dense = mesh.shape["dp"] == 2 and mesh.shape["expert"] == 16
         return (dense_body if dense else body)(tokens, *others)
 
     return chosen

time: 324 us -> 277 us (0.85)
  Pallas kernels: 0 us -> 114 us
  waiting for transfers between devices: 176 us -> 70.4 us
  starting transfers between devices: 35.8 us -> 0.52 us
  blocking collectives: 52 us -> 43.6 us
  other arithmetic: 7.21 us -> 1.79 us
  local copies, waits for them, and re-layouts: 17.6 us -> 14.3 us
    all_to_all x5 -> x0, waiting for transfers between devices: 147 us -> none  [the longest x2 61.2 us: move_slots(): lax.all_to_all(picked, 'expert', split_axis=0, concat_axis=0, tiled=True)]
    pallas_call x0 -> x1, Pallas kernels: none -> 114 us  [swap_and_return(): pl.pallas_call(swap_kernel, out_shape=(jax.ShapeDtypeStruct(up_shape, kin...]
    all_gather x1, waiting for transfers between devices: 26.7 us -> 70.4 us  [dense_body(): every = lax.all_gather(both, 'expert', axis=1, tiled=True)]
    all_to_all x5 -> x0, starting transfers between devices: 35.2 us -> none  [the longest x2 15.3 us: move_slots(): lax.all_to_all(picked, 'expert', split_axis=0, concat_axis=0, tiled=True)]
    gather x2 -> x0, local copies, waits for them, and re-layouts: 6.4 us -> none  [move_slots(): picked = jnp.take(spread, partner, axis=0)]
    select_n x3 -> x2, other arithmetic: 5.54 us -> 0.1 us  [the longest x1 0.09 us: route_table(): cross_at = source % 4]
    all_gather x1, blocking collectives: 44.2 us -> 39.7 us  [dense_body(): lax.all_gather(by_slot, ('expert', 'dp'), axis=0, tiled=True)]
    all_to_all x1 -> x0, blocking collectives: 3.78 us -> none  [dense_body(): lax.all_to_all(summed, 'dp', split_axis=0, concat_axis=1, tiled=True)]
  transfers between devices with their start and end apart: 8 -> 3, of which waited for: 8 -> 1; matrix products, arithmetic and copies ran while one was open for 8% -> 5% of each run, Pallas kernels for 0% -> 0%
where the time goes in v2:
time: 277 us
  Pallas kernels  114 us (41%)
  waiting for transfers between devices  70.4 us (25%)
  blocking collectives  43.6 us (16%)
  matrix products  18.1 us (7%)
  local copies, waits for them, and re-layouts  14.3 us (5%)
  between operations  14.3 us (5%)
    pallas_call x1, Pallas kernels, swap_and_return(): pl.pallas_call(swap_kernel, out_shape=(jax.ShapeDtypeStruct(up_shape, kin...  114 us
    all_gather x1, waiting for transfers between devices, dense_body(): every = lax.all_gather(both, 'expert', axis=1, tiled=True)  70.4 us
    all_gather x1, blocking collectives, dense_body(): lax.all_gather(by_slot, ('expert', 'dp'), axis=0, tiled=True)  39.7 us
    unnamed x24, local copies, waits for them, and re-layouts  9.67 us
  transfers between devices with their start and end apart: 3, of which 1 were waited for; matrix products, arithmetic and copies ran while one was open for 5% of the time, Pallas kernels for 0%

profile of v2, /device:TPU:0, one launch (start us, length us, event | category | flops | bytes accessed | tf_op | source)
XLA Modules:
  0.0 277.1 jit_solution(10257110558570918816)
XLA Ops:
  7.2 0.0 copy-start
  7.2 0.0 all-gather.3.cloned.1.call-start
  7.2 1.1 pad_maximum_fusion
  8.3 0.7 copy.32
  9.0 0.0 copy-start.2
  9.1 0.0 copy-start.3
  9.1 0.0 copy-start.4
  9.1 0.0 copy-start.5
  9.1 1.4 reshape.84
  10.5 3.9 %all_to_all.18 = bf16[2,2,24576]{2,1,0:T(2,128)(2,1)S(1)} all-to-all(bf16[2,2,24576]{2,1,0:T(2,128)(2,1)S(1)} %reshape.84), channel_id=1, replica_groups=mesh['expert'=16,'dp'=2] {'dp'}, dimensions={0} | all-to-all | bytes 393216 | tf_op jit(solution)/shard_map/all_to_all | solution.py:481
  14.4 1.5 reshape.85
  15.8 1.7 copy.33
  17.6 0.0 all-gather.3.cloned.1.call-update
  17.6 0.0 copy-done.2
  17.7 0.1 reshape.80
  17.7 0.2 reduce_window_sum.11
  17.9 0.1 sub.39
  18.0 0.0 copy-done.3
  18.0 0.0 copy-done.4
  18.0 0.0 copy-done.5
  18.1 0.1 iota_compare_fusion.1
  18.1 0.1 select_reduce_fusion
  18.3 70.4 %all-gather.3.cloned.1.call-done = bf16[2,768,1024]{2,1,0:T(8,128)(2,1)} async-done(((bf16[2,48,1024]{2,1,0:T(8,128)(2,1)}), bf16[2,768,1024]{2,1,0:T(8,128)(2,1)}) %all-gather.3.cloned.1.call-update) | async-done | bytes 3145744 | tf_op jit(solution)/shard_map/all_gather | solution.py:484
  88.6 3.3 %fusion.15 = bf16[768,768]{1,0:T(8,128)(2,1)S(1)} fusion(bf16[1,1024,768]{2,1,0:T(8,128)(2,1)} %param.16, bf16[2,768,1024]{2,1,0:T(8,128)(2,1)} %all-gather.3.cloned.1.call-done), kind=kOutput, calls=%fused_computation.25 | convolution fusion | flops 1208549376 | bytes 4325376 | tf_op jit(solution)/shard_map/dot_general | solution.py:488
  91.9 0.1 collective-permute-start.1
  92.0 39.7 %all-gather = f32[32,24,16]{1,2,0:T(8,128)S(1)} all-gather(f32[1,24,16]{1,2,0:T(8,128)S(1)} %bitcast.68), channel_id=1, replica_groups=mesh['expert'=16,'dp'=2] {'expert','dp'}, dimensions={0}, use_global_device_ids=true | all-gather | bytes 50688 | tf_op jit(solution)/shard_map/all_gather | solution.py:477
  131.7 0.1 copy.34
  131.8 0.2 reshape.83
  132.0 0.1 select_reduce_fusion.3
  132.1 0.1 and_select_fusion.4
  132.2 0.6 concatenate.3.refs_0_
  132.8 0.1 select_reduce_fusion.2
  132.9 0.0 copy-done
  132.9 2.8 %fusion.18 = bf16[768,768]{1,0:T(8,128)(2,1)S(1)} fusion(bf16[1,768,1024]{2,1,0:T(8,128)(2,1)S(1)} %copy-done, f32[768]{0:T(1024)S(1)} %select_reduce_fusion.2, bf16[2,768,1024]{2,1,0:T(8,128)(2,1)} %all-gather.3.cloned.1.call-done), kind=kOutput, calls=%fused_computation.26 | convolution fusion | flops 1210908672 | bytes 4328448 | tf_op jit(solution)/shard_map/dot_general | solution.py:489
  135.8 0.4 collective-permute-start
  136.2 0.0 collective-permute-done.1
  136.2 0.0 copy-start.7
  136.2 2.9 %multiply_convert_fusion = bf16[768,1024]{1,0:T(8,128)(2,1)S(1)} fusion(f32[768]{0:T(1024)S(1)} %select_reduce_fusion.2, bf16[1,768,1024]{2,1,0:T(8,128)(2,1)S(1)} %copy-done, bf16[768,768]{1,0:T(8,128)(2,1)} %collective-permute-done.1, bf16[768,768]{1,0:T(8,128)(2,1)S(1)} %fusion.15), kind=kOutput, calls=%fused_computation.9 | convolution fusion | flops 1215823872 | bytes 5508096 | tf_op jit(solution)/shard_map/dot_general | solution.py:512
  139.1 0.0 copy-start.6
  139.1 1.3 copy.37
  140.4 0.0 copy-done.7
  140.4 1.2 copy-done.6
  141.6 0.0 copy-start.8
  141.6 4.5 %fusion.3 = bf16[768,1024]{1,0:T(8,128)(2,1)} fusion(bf16[1,768,1024]{2,1,0:T(8,128)(2,1)S(1)} %copy-done.7, f32[768]{0:T(1024)S(1)} %select_reduce_fusion.2, bf16[2,768,1024]{2,1,0:T(8,128)(2,1)S(1)} %copy-done.6, bf16[768,768]{1,0:T(8,128)(2,1)} %collective-permute-done.1, bf16[768,768]{1,0:T(8,128)(2,1)S(1)} %fusion.15), kind=kOutput, calls=%fused_computation.6 | convolution fusion | flops 1218969600 | bytes 7081984 | tf_op jit(solution)/shard_map/dot_general | solution.py:506
  146.0 0.0 collective-permute-done
  146.0 0.0 copy-done.8
  146.0 4.6 %fusion.4 = bf16[1024,768]{1,0:T(8,128)(2,1)} fusion(bf16[1,1024,768]{2,1,0:T(8,128)(2,1)S(1)} %copy-done.8, bf16[2,768,1024]{2,1,0:T(8,128)(2,1)S(1)} %copy-done.6, bf16[768,768]{1,0:T(8,128)(2,1)S(1)} %collective-permute-done, bf16[768,768]{1,0:T(8,128)(2,1)S(1)} %fusion.18, bf16[768,768]{1,0:T(8,128)(2,1)} %collective-permute-done.1, ...), kind=kOutput, calls=%fused_computation.8 | convolution fusion | flops 1220739072 | bytes 9437184 | tf_op jit(solution)/shard_map/dot_general | solution.py:500
  150.6 114.1 %shard_map.121 = (bf16[4,4,64,768]{3,2,1,0:T(8,128)(2,1)}, bf16[4,4,48,1024]{3,2,1,0:T(8,128)(2,1)}, bf16[24,2048]{1,0:T(8,128)(2,1)}) custom-call(s32[24]{0:T(128)} %concatenate.3.refs_0_, bf16[4,4,64,768]{3,2,1,0:T(8,128)(2,1)} %bitcast.61, bf16[4,4,48,1024]{3,2,1,0:T(8,128)(2,1)} %bitcast.60, bf16[4,4,2,24,1024]{4,3,2,1,0:T(8,128)(2,1)} %bitcast.57), custom_call_target="tpu_custom_call" | custom-call | tf_op jit(solution)/shard_map/pallas_call | solution.py:412
  264.7 0.0 copy-start.1
  264.8 1.7 copy.41
  266.4 2.7 copy.42
  269.1 0.0 copy-done.1
  269.1 1.1 copy.43
  (7 shorter events, 0.1 us)
Async XLA Ops:
  7.2 125.7 %copy-start = (bf16[1,768,1024]{2,1,0:T(8,128)(2,1)S(1)}, bf16[1,768,1024]{2,1,0:T(8,128)(2,1)}, u32[]{:S(2)}) copy-start(bf16[1,768,1024]{2,1,0:T(8,128)(2,1)} %param.17) | copy-start | bytes 4718596
  7.2 81.4 %all-gather.3.cloned.1.call-start = ((), (), s32[]{:S(2)}) async-start(), calls=%async_computation.1 | async-start | bytes 3342336 | tf_op jit(solution)/shard_map/all_gather | solution.py:484
  9.0 8.6 %copy-start.2 = (s32[16]{0:T(128)S(1)}, s32[16]{0:T(128)}, u32[]{:S(2)}) copy-start(s32[16]{0:T(128)} %param.15) | copy-start | bytes 196
  9.1 9.0 %copy-start.3 = (f32[24,8]{0,1:T(8,128)S(1)}, f32[24,8]{0,1:T(8,128)}, u32[]{:S(2)}) copy-start(f32[24,8]{0,1:T(8,128)} %param.12) | copy-start | bytes 2308
  9.1 9.0 %copy-start.4 = (s32[24,8]{0,1:T(8,128)S(1)}, s32[24,8]{0,1:T(8,128)}, u32[]{:S(2)}) copy-start(s32[24,8]{0,1:T(8,128)} %param.11) | copy-start | bytes 2308
  9.1 9.0 %copy-start.5 = (s32[16]{0:T(128)S(1)}, s32[16]{0:T(128)}, u32[]{:S(2)}) copy-start(s32[16]{0:T(128)} %param.14) | copy-start | bytes 196
  91.9 44.3 %collective-permute-start.1 = (bf16[768,768]{1,0:T(8,128)(2,1)S(1)}, bf16[768,768]{1,0:T(8,128)(2,1)}, u32[]{:S(2)}, u32[]{:S(2)}) collective-permute-start(bf16[768,768]{1,0:T(8,128)(2,1)S(1)} %fusion.15), channel_id=1, source_target_pairs={{0,1},{1,0},{2,3},{3,2},{4,5},{5,4},{6,7},{7,6},{8,9},{9,8},{10,11... | collective-permute-start | bytes 3538952 | tf_op jit(solution)/shard_map/ppermute | solution.py:492
  135.8 10.3 %collective-permute-start = (bf16[768,768]{1,0:T(8,128)(2,1)S(1)}, bf16[768,768]{1,0:T(8,128)(2,1)S(1)}, u32[]{:S(2)}, u32[]{:S(2)}) collective-permute-start(bf16[768,768]{1,0:T(8,128)(2,1)S(1)} %fusion.18), channel_id=1, source_target_pairs={{0,1},{1,0},{2,3},{3,2},{4,5},{5,4},{6,7},{7,6},{8,9},{9,8},{10,11... | collective-permute-start | bytes 3538952 | tf_op jit(solution)/shard_map/ppermute | solution.py:495
  136.2 4.2 %copy-start.7 = (bf16[1,768,1024]{2,1,0:T(8,128)(2,1)S(1)}, bf16[1,768,1024]{2,1,0:T(8,128)(2,1)}, u32[]{:S(2)}) copy-start(bf16[1,768,1024]{2,1,0:T(8,128)(2,1)} %param.19) | copy-start | bytes 4718596
  139.1 2.5 copy-start.6
  141.6 4.5 %copy-start.8 = (bf16[1,1024,768]{2,1,0:T(8,128)(2,1)S(1)}, bf16[1,1024,768]{2,1,0:T(8,128)(2,1)}, u32[]{:S(2)}) copy-start(bf16[1,1024,768]{2,1,0:T(8,128)(2,1)} %param.18) | copy-start | bytes 4718596
  264.7 4.3 %copy-start.1 = (bf16[4,4,48,1024]{3,2,1,0:T(8,128)(2,1)S(1)}, bf16[4,4,48,1024]{3,2,1,0:T(8,128)(2,1)}, u32[]{:S(2)}) copy-start(bf16[4,4,48,1024]{3,2,1,0:T(8,128)(2,1)} %get-tuple-element.8) | copy-start | bytes 4718596
Sparse Core Ops, SparseCore 0:
  17.7 70.8 all-gather.2

commit v3 on v2

--- a/solution.py
+++ b/solution.py
@@ -456,6 +456,131 @@
     )
 
 
+def gather_kernel(*refs):
+    arrays, ends = refs[:3], refs[3:6]
+    line_send, line_recv, near_send, near_recv, far_send, far_recv = refs[6:]
+    me = lax.axis_index("expert")
+    core = lax.axis_index("dp")
+    z, spot = me // 4, me % 4
+    near = [z * 4 + lax.bitwise_xor(spot, r) for r in (1, 2)]
+    line = [lax.bitwise_xor(z, r) * 4 + spot for r in range(4)]
+    hops = [(r, flip) for r in (0, 1, 2, 3) for flip in (0, 1) if r + flip > 0]
+
+    barrier = pltpu.get_barrier_semaphore()
+    for r, flip in hops:
+        pl.semaphore_signal(
+            barrier,
+            inc=1,
+            device_id=(line[r], lax.bitwise_xor(core, flip)),
+            device_id_type=MESH,
+        )
+    for peer in near:
+        pl.semaphore_signal(barrier, inc=1, device_id=(peer, core), device_id_type=MESH)
+    pl.semaphore_wait(barrier, len(hops) + 2)
+
+    def line_copy(a, r, flip):
+        at_core = lax.bitwise_xor(core, flip)
+        return pltpu.make_async_remote_copy(
+            src_ref=arrays[a] if a == 2 else arrays[a].at[at_core],
+            dst_ref=ends[a].at[me, core],
+            send_sem=line_send.at[a, r * 2 + flip],
+            recv_sem=line_recv.at[a, r * 2 + flip],
+            device_id=(line[r], at_core),
+            device_id_type=MESH,
+        )
+
+    def near_copy(a, r, way):
+        block = ends[a].at[line[r]]
+        return pltpu.make_async_remote_copy(
+            src_ref=block,
+            dst_ref=block,
+            send_sem=near_send.at[a, r, way],
+            recv_sem=near_recv.at[a, r, way],
+            device_id=(near[way], core),
+            device_id_type=MESH,
+        )
+
+    def far_copy(a, r):
+        came = 1 if a == 1 else 0
+        block = ends[a].at[lax.bitwise_xor(z, r) * 4 + lax.bitwise_xor(spot, came + 1)]
+        return pltpu.make_async_remote_copy(
+            src_ref=block,
+            dst_ref=block,
+            send_sem=far_send.at[a, r],
+            recv_sem=far_recv.at[a, r],
+            device_id=(near[1 - came], core),
+            device_id_type=MESH,
+        )
+
+    for r, flip in hops:
+        for a in range(3):
+            line_copy(a, r, flip).start()
+    for a in range(2):
+        ends[a][me, core] = arrays[a][core]
+    ends[2][me, core] = arrays[2][...]
+
+    for step in range(5):
+        if step < 4:
+            for a in range(3):
+                for flip in (0, 1):
+                    if step + flip > 0:
+                        line_copy(a, step, flip).wait_recv()
+                for way in (0, 1):
+                    near_copy(a, step, way).start()
+        if step >= 1:
+            for a in range(3):
+                came = 1 if a == 1 else 0
+                near_copy(a, step - 1, came).wait_recv()
+                far_copy(a, step - 1).start()
+
+    for a in range(3):
+        for r in range(4):
+            near_copy(a, r, 0 if a == 1 else 1).wait_recv()
+            far_copy(a, r).wait_recv()
+            far_copy(a, r).wait_send()
+            for way in (0, 1):
+                near_copy(a, r, way).wait_send()
+        for r, flip in hops:
+            line_copy(a, r, flip).wait_send()
+
+
+def gather_tokens(tokens, cotangent, by_slot, me):
+    tok_count, feature_count = tokens.shape
+    half = feature_count // 2
+    kind = tokens.dtype
+
+    def by_half(array_item):
+        return array_item.reshape(tok_count, 2, half).transpose(1, 0, 2)
+
+    flat = by_slot.T.reshape(-1, 128)
+    table_rows = flat.shape[0]
+    flat = jnp.pad(flat, ((0, 8 - table_rows), (0, 0)))
+    vmem = pl.BlockSpec(memory_space=pltpu.VMEM)
+    dma = pltpu.SemaphoreType.DMA
+    full = jax.ShapeDtypeStruct((16, 2, tok_count, half), kind)
+    rows, cots, tables = pl.pallas_call(
+        gather_kernel,
+        out_shape=(full, full, jax.ShapeDtypeStruct((16, 2, 8, 128), jnp.float32)),
+        in_specs=[vmem] * 3,
+        out_specs=(vmem,) * 3,
+        scratch_shapes=[
+            dma((3, 8)),
+            dma((3, 8)),
+            dma((3, 4, 2)),
+            dma((3, 4, 2)),
+            dma((3, 4)),
+            dma((3, 4)),
+        ],
+        compiler_params=pltpu.CompilerParams(
+            collective_id=2, has_side_effects=True, vmem_limit_bytes=32 * 1024 * 1024
+        ),
+    )(by_half(tokens), by_half(cotangent), flat)
+    weights = tables[:, :, :table_rows].reshape(32, 16, tok_count)
+    hit = jnp.arange(16)[None, :, None] == me
+    scale = jnp.sum(jnp.where(hit, weights, 0.0), axis=1).reshape(-1, 1)
+    return rows.reshape(-1, half), cots.reshape(-1, half), scale
+
+
 def dense_body(
     tokens,
     expert_ids,
@@ -469,20 +594,10 @@
     down_moment,
 ):
     n_slots = lax.axis_size("expert")
-    tok_count, feature_count = tokens.shape
-    half = feature_count // 2
     swap_pair = [(0, 1), (1, 0)]
     me = lax.axis_index("expert")
     by_slot = own_weights(expert_ids, route_weight, holder, n_slots)
-    gathered_weights = lax.all_gather(by_slot, ("expert", "dp"), axis=0, tiled=True)
-    scale = jnp.sum(
-        jnp.where(jnp.arange(n_slots)[None, :] == me, gathered_weights, 0.0), axis=1, keepdims=True
-    )
-    both = lax.all_to_all(
-        jnp.stack([tokens, cotangent]), "dp", split_axis=2, concat_axis=1, tiled=True
-    )
-    every = lax.all_gather(both, "expert", axis=1, tiled=True)
-    rows, cots = every[0], every[1]
+    rows, cots, scale = gather_tokens(tokens, cotangent, by_slot, me)
     grads = (scale * cots.astype(jnp.float32)).astype(jnp.bfloat16)
     up_local, down_local = up_weight[0], down_weight[0]
     pre_part = jnp.dot(rows, up_local, preferred_element_type=jnp.float32).astype(jnp.bfloat16)

time: 277 us -> 189 us (0.68)
  waiting for transfers between devices: 70.4 us -> 1.19 us
  blocking collectives: 43.6 us -> 0 us
  Pallas kernels: 114 us -> 154 us
  between operations: 14.3 us -> 0.82 us
  local copies, waits for them, and re-layouts: 14.3 us -> 11.1 us
    all_gather x1 -> x0, waiting for transfers between devices: 70.4 us -> none  [dense_body(): every = lax.all_gather(both, 'expert', axis=1, tiled=True)]
    pallas_call x0 -> x1, Pallas kernels: none -> 40.2 us  [gather_tokens(): pl.pallas_call(gather_kernel, out_shape=(full, full, jax.ShapeDtypeStruct...]
    all_gather x1 -> x0, blocking collectives: 39.7 us -> none  [dense_body(): lax.all_gather(by_slot, ('expert', 'dp'), axis=0, tiled=True)]
    all_to_all x1 -> x0, blocking collectives: 3.89 us -> none  [dense_body(): lax.all_to_all(jnp.stack([tokens, cotangent]), 'dp', split_axis=2, concat...]
    unnamed x24 -> x21, local copies, waits for them, and re-layouts: 9.67 us -> 7.78 us
  transfers between devices with their start and end apart: 3 -> 2, of which waited for: 1 -> 1; matrix products, arithmetic and copies ran while one was open for 5% -> 4% of each run, Pallas kernels for 0% -> 0%
where the time goes in v3:
time: 189 us
  Pallas kernels  154 us (81%)
  matrix products  18.1 us (10%)
  local copies, waits for them, and re-layouts  11.1 us (6%)
  other arithmetic  2.87 us (2%)
    pallas_call x1, Pallas kernels, swap_and_return(): pl.pallas_call(swap_kernel, out_shape=(jax.ShapeDtypeStruct(up_shape, kin...  114 us
    pallas_call x1, Pallas kernels, gather_tokens(): pl.pallas_call(gather_kernel, out_shape=(full, full, jax.ShapeDtypeStruct...  40.2 us
    unnamed x21, local copies, waits for them, and re-layouts  7.78 us
    dot_general x1, matrix products, dense_body(): lax.dot_general(rows, pre_grad, (((0,), (0,)), ((), ())), preferred_eleme...  5.68 us
    dot_general x1, matrix products, dense_body(): lax.dot_general(hidden, grads, (((0,), (0,)), ((), ())), preferred_elemen...  4.46 us
  transfers between devices with their start and end apart: 2, of which 1 were waited for; matrix products, arithmetic and copies ran while one was open for 4% of the time, Pallas kernels for 0%

profile of v3, /device:TPU:0, one launch (start us, length us, event | category | flops | bytes accessed | tf_op | source)
XLA Modules:
  0.0 188.7 jit_solution(6803937505955654043)
XLA Ops:
  0.6 0.0 copy-start
  0.7 0.8 iota_compare_fusion.1
  1.5 0.7 select_reduce_fusion.2
  2.2 0.1 select_reduce_fusion.1
  2.3 0.1 reshape.94
  2.4 1.0 bitcast_bitcast_fusion
  3.4 40.2 %shard_map.121 = (bf16[16,2,24,1024]{3,2,1,0:T(8,128)(2,1)S(1)}, bf16[16,2,24,1024]{3,2,1,0:T(8,128)(2,1)S(1)}, f32[16,2,8,128]{3,2,1,0:T(8,128)S(1)}) custom-call(bf16[2,24,1024]{2,1,0:T(8,128)(2,1)S(1)} %get-tuple-element.30.refs_0_, bf16[2,24,1024]{2,1,0:T(8,128)(2,1)S(1)} %get-tuple-element.29.refs_1_, f32[8,128]{1,0:T(8,128)S(1)} %pad.4.refs_2_), custom_call_target="tpu_custom_call" | custom-call | tf_op jit(solution)/shard_map/pallas_call | solution.py:561
  43.6 0.0 copy-start.1
  43.6 1.1 copy-done.1
  44.7 0.2 reshape.96
  44.9 0.1 select_reduce_fusion
  45.0 0.3 multiply_convert_fusion.1
  45.4 0.0 copy-done
  45.4 0.0 copy-start.2
  45.4 0.0 copy-start.6
  45.4 2.4 %fusion.8 = bf16[768,768]{1,0:T(8,128)(2,1)} fusion(bf16[768,1024]{1,0:T(8,128)(2,1)S(1)} %bitcast.60, bf16[1,768,1024]{2,1,0:T(8,128)(2,1)S(1)} %copy-done), kind=kOutput, calls=%fused_computation.19 | convolution fusion | flops 1208549376 | bytes 4325376 | tf_op jit(solution)/shard_map/dot_general | solution.py:604
  47.9 0.0 collective-permute-start
  47.9 0.0 copy-done.2
  47.9 0.0 copy-done.6
  47.9 0.0 copy-start.5
  47.9 2.4 %fusion.11 = bf16[768,768]{1,0:T(8,128)(2,1)} fusion(bf16[768,1024]{1,0:T(8,128)(2,1)S(1)} %bitcast.52, bf16[1,1024,768]{2,1,0:T(8,128)(2,1)S(1)} %copy-done.6), kind=kOutput, calls=%fused_computation.20 | convolution fusion | flops 1208549376 | bytes 4325376 | tf_op jit(solution)/shard_map/dot_general | solution.py:603
  50.3 0.5 collective-permute-start.1
  50.8 0.0 copy-done.5
  50.8 0.1 reshape.102
  50.9 0.2 reduce_window_sum.11
  51.1 0.1 mul.91
  51.2 0.1 sub.39
  51.3 0.1 select_reduce_fusion.3
  51.4 0.1 and_select_fusion.4
  51.5 0.6 concatenate.3.refs_0_
  52.1 0.3 fusion
  52.4 1.2 collective-permute-done.1
  53.6 3.1 %multiply_convert_fusion = bf16[768,1024]{1,0:T(8,128)(2,1)S(1)} fusion(f32[768]{0:T(1024)S(1)} %mul.91, bf16[1,768,1024]{2,1,0:T(8,128)(2,1)S(1)} %copy-done, bf16[768,768]{1,0:T(8,128)(2,1)} %collective-permute-done.1, bf16[768,768]{1,0:T(8,128)(2,1)} %fusion.11), kind=kOutput, calls=%fused_computation.6 | convolution fusion | flops 1215823872 | bytes 5508096 | tf_op jit(solution)/shard_map/dot_general | solution.py:627
  56.8 0.0 copy-start.3
  56.8 0.0 copy-start.7
  56.8 1.3 copy.28
  58.1 0.0 copy-start.8
  58.1 0.0 collective-permute-done
  58.1 0.7 copy-done.3
  58.7 0.5 copy-done.7
  59.2 5.7 %fusion.2 = bf16[1024,768]{1,0:T(8,128)(2,1)} fusion(bf16[1,1024,768]{2,1,0:T(8,128)(2,1)S(1)} %copy-done.7, bf16[768,1024]{1,0:T(8,128)(2,1)S(1)} %bitcast.53, bf16[768,768]{1,0:T(8,128)(2,1)} %collective-permute-done, bf16[768,768]{1,0:T(8,128)(2,1)} %fusion.8, bf16[768,768]{1,0:T(8,128)(2,1)} %collective-permute-done.1, bf16[768,768]{1,0:T(8,128)(2,1)} %fusion.11), kind=kOutput, calls=%fused_computation.5 | convolution fusion | flops 1220739072 | bytes 9437184 | tf_op jit(solution)/shard_map/dot_general | solution.py:615
  64.9 0.0 copy-done.8
  64.9 4.5 %fusion.1 = bf16[768,1024]{1,0:T(8,128)(2,1)} fusion(bf16[1,768,1024]{2,1,0:T(8,128)(2,1)S(1)} %copy-done.8, bf16[768,1024]{1,0:T(8,128)(2,1)S(1)} %fusion, bf16[768,768]{1,0:T(8,128)(2,1)} %collective-permute-done.1, bf16[768,768]{1,0:T(8,128)(2,1)} %fusion.11), kind=kOutput, calls=%fused_computation.3 | convolution fusion | flops 1216610304 | bytes 7077888 | tf_op jit(solution)/shard_map/dot_general | solution.py:621
  69.3 113.9 %shard_map.122 = (bf16[4,4,64,768]{3,2,1,0:T(8,128)(2,1)}, bf16[4,4,48,1024]{3,2,1,0:T(8,128)(2,1)}, bf16[24,2048]{1,0:T(8,128)(2,1)}) custom-call(s32[24]{0:T(128)} %concatenate.3.refs_0_, bf16[4,4,64,768]{3,2,1,0:T(8,128)(2,1)} %bitcast.55, bf16[4,4,48,1024]{3,2,1,0:T(8,128)(2,1)} %bitcast.56, bf16[4,4,2,24,1024]{4,3,2,1,0:T(8,128)(2,1)} %bitcast.54), custom_call_target="tpu_custom_call" | custom-call | tf_op jit(solution)/shard_map/pallas_call | solution.py:412
  183.2 1.5 copy.32
  184.8 0.0 copy-start.4
  184.8 2.8 %copy.33 = bf16[1,1024,768]{2,1,0:T(8,128)(2,1)} copy(bf16[1,1024,768]{2,1,0:T(8,128)(2,1)} %bitcast.58) | data formatting | bytes 3145728
  187.6 0.0 copy-done.4
  187.6 1.1 copy.34
  (8 shorter events, 0.1 us)
Async XLA Ops:
  0.6 44.7 %copy-start = (bf16[1,768,1024]{2,1,0:T(8,128)(2,1)S(1)}, bf16[1,768,1024]{2,1,0:T(8,128)(2,1)}, u32[]{:S(2)}) copy-start(bf16[1,768,1024]{2,1,0:T(8,128)(2,1)} %param.17) | copy-start | bytes 4718596
  43.6 1.1 copy-start.1
  45.4 2.5 %copy-start.2 = (bf16[16,2,24,1024]{3,2,1,0:T(8,128)(2,1)S(1)}, bf16[16,2,24,1024]{3,2,1,0:T(8,128)(2,1)}, u32[]{:S(2)}) copy-start(bf16[16,2,24,1024]{3,2,1,0:T(8,128)(2,1)} %copy-done.1) | copy-start | bytes 4718596
  45.4 2.5 %copy-start.6 = (bf16[1,1024,768]{2,1,0:T(8,128)(2,1)S(1)}, bf16[1,1024,768]{2,1,0:T(8,128)(2,1)}, u32[]{:S(2)}) copy-start(bf16[1,1024,768]{2,1,0:T(8,128)(2,1)} %param.16) | copy-start | bytes 4718596
  47.9 10.2 %collective-permute-start = (bf16[768,768]{1,0:T(8,128)(2,1)}, bf16[768,768]{1,0:T(8,128)(2,1)}, u32[]{:S(2)}, u32[]{:S(2)}) collective-permute-start(bf16[768,768]{1,0:T(8,128)(2,1)} %fusion.8), channel_id=1, source_target_pairs={{0,1},{1,0},{2,3},{3,2},{4,5},{5,4},{6,7},{7,6},{8,9},{9,8},{10,11... | collective-permute-start | bytes 3538952 | tf_op jit(solution)/shard_map/ppermute | solution.py:610
  47.9 2.9 %copy-start.5 = (s32[16]{0:T(128)S(1)}, s32[16]{0:T(128)}, u32[]{:S(2)}) copy-start(s32[16]{0:T(128)} %param.15) | copy-start | bytes 196
  50.3 3.3 %collective-permute-start.1 = (bf16[768,768]{1,0:T(8,128)(2,1)}, bf16[768,768]{1,0:T(8,128)(2,1)}, u32[]{:S(2)}, u32[]{:S(2)}) collective-permute-start(bf16[768,768]{1,0:T(8,128)(2,1)} %fusion.11), channel_id=1, source_target_pairs={{0,1},{1,0},{2,3},{3,2},{4,5},{5,4},{6,7},{7,6},{8,9},{9,8},{10,11... | collective-permute-start | bytes 3538952 | tf_op jit(solution)/shard_map/ppermute | solution.py:607
  56.8 2.0 %copy-start.3 = (bf16[16,2,24,1024]{3,2,1,0:T(8,128)(2,1)S(1)}, bf16[16,2,24,1024]{3,2,1,0:T(8,128)(2,1)}, u32[]{:S(2)}) copy-start(bf16[16,2,24,1024]{3,2,1,0:T(8,128)(2,1)} %copy-done.1) | copy-start | bytes 4718596
  56.8 2.4 %copy-start.7 = (bf16[1,1024,768]{2,1,0:T(8,128)(2,1)S(1)}, bf16[1,1024,768]{2,1,0:T(8,128)(2,1)}, u32[]{:S(2)}) copy-start(bf16[1,1024,768]{2,1,0:T(8,128)(2,1)} %param.18) | copy-start | bytes 4718596
  58.1 6.8 %copy-start.8 = (bf16[1,768,1024]{2,1,0:T(8,128)(2,1)S(1)}, bf16[1,768,1024]{2,1,0:T(8,128)(2,1)}, u32[]{:S(2)}) copy-start(bf16[1,768,1024]{2,1,0:T(8,128)(2,1)} %param.19) | copy-start | bytes 4718596
  184.8 2.8 %copy-start.4 = (bf16[4,4,48,1024]{3,2,1,0:T(8,128)(2,1)S(1)}, bf16[4,4,48,1024]{3,2,1,0:T(8,128)(2,1)}, u32[]{:S(2)}) copy-start(bf16[4,4,48,1024]{3,2,1,0:T(8,128)(2,1)} %get-tuple-element.14) | copy-start | bytes 4718596

commit v4 on v3

--- a/solution.py
+++ b/solution.py
@@ -139,7 +139,10 @@
 
 
 MESH = pl.DeviceIdType.MESH
-CHUNKS = 4
+UP_CHUNKS = 8
+DOWN_CHUNKS = 6
+CHUNKS = UP_CHUNKS + DOWN_CHUNKS
+AHEAD = 2
 
 
 def route_table(partner, me):
@@ -179,7 +182,7 @@
 def swap_kernel(*refs):
     table, new_up, new_down, outs, up_end, down_end, layer = refs[:7]
     scratch = list(refs[7:])
-    total = 2 * CHUNKS
+    total = CHUNKS
 
     def take(number):
         taken = scratch[:number]
@@ -218,8 +221,9 @@
     pl.semaphore_signal(barrier, inc=1, device_id=(me, 1 - core), device_id_type=MESH)
     pl.semaphore_wait(barrier, 7)
 
-    sources = [new_up] * CHUNKS + [new_down] * CHUNKS
-    ends = [up_end] * CHUNKS + [down_end] * CHUNKS
+    sources = [new_up] * UP_CHUNKS + [new_down] * DOWN_CHUNKS
+    ends = [up_end] * UP_CHUNKS + [down_end] * DOWN_CHUNKS
+    places = list(range(UP_CHUNKS)) + list(range(DOWN_CHUNKS))
 
     def remote(src, dst, send, recv, peer, at_core=None):
         return pltpu.make_async_remote_copy(
@@ -233,7 +237,7 @@
 
     def spread(k, r):
         return remote(
-            sources[k].at[lax.bitwise_xor(spot, r), k % CHUNKS],
+            sources[k].at[lax.bitwise_xor(spot, r), places[k]],
             own[k].at[spot],
             spread_send.at[k, r - 1],
             spread_recv.at[k, r - 1],
@@ -243,7 +247,7 @@
     def finish(k, r):
         return remote(
             final[k].at[lax.bitwise_xor(spot, r)],
-            ends[k].at[spot, k % CHUNKS],
+            ends[k].at[spot, places[k]],
             end_send.at[k, r - 1],
             end_recv.at[k, r - 1],
             plane_peers[r - 1],
@@ -290,7 +294,7 @@
     def begin(k):
         for r in (1, 2, 3):
             spread(k, r).start()
-        own[k][spot] = sources[k][spot, k % CHUNKS]
+        own[k][spot] = sources[k][spot, places[k]]
 
     def stage_first(k):
         for r in (1, 2, 3):
@@ -326,25 +330,26 @@
     def send_final(k):
         for r in (1, 2, 3):
             finish(k, r).start()
-        ends[k][spot, k % CHUNKS] = final[k][spot]
-
-    for k in range(CHUNKS):
-        begin(k)
-    for r in (1, 2, 3):
-        plane_copy(r).start()
-    for k in range(CHUNKS, total):
+        ends[k][spot, places[k]] = final[k][spot]
+
+    for k in range(AHEAD):
         begin(k)
 
     for step in range(total + 3):
         if step < total:
             stage_first(step)
+        if step + AHEAD < total:
+            begin(step + AHEAD)
+        if step == 0:
+            for r in (1, 2, 3):
+                plane_copy(r).start()
         if 0 <= step - 1 < total:
             stage_cross(step - 1)
         if 0 <= step - 2 < total:
             stage_pass(step - 2)
         if 0 <= step - 3 < total:
             stage_outer(step - 3)
-        if step == CHUNKS:
+        if step == 7:
             for r in (1, 2, 3):
                 plane_copy(r).wait_recv()
 
@@ -358,7 +363,7 @@
 
             for r in (1, 2, 3):
                 line_copy(r).start()
-        if step == CHUNKS + 3:
+        if step == 11:
             for r in (1, 2, 3):
                 line_copy(r).wait_recv()
             for group in range(2):
@@ -397,14 +402,15 @@
 def swap_and_return(new_up, new_down, outs, partner, me):
     half, hidden_count = new_up.shape
     tok_count = outs.shape[0] // 32
-    up_rows, down_rows = half // (4 * CHUNKS), hidden_count // (4 * CHUNKS)
-    up_shape = (4, CHUNKS, up_rows, hidden_count)
-    down_shape = (4, CHUNKS, down_rows, half)
+    up_rows = half // (4 * UP_CHUNKS)
+    down_rows = hidden_count // (4 * DOWN_CHUNKS)
+    up_shape = (4, UP_CHUNKS, up_rows, hidden_count)
+    down_shape = (4, DOWN_CHUNKS, down_rows, half)
     kind = new_up.dtype
-    pieces = [pltpu.VMEM((4,) + up_shape[2:], kind)] * CHUNKS + [
+    pieces = [pltpu.VMEM((4,) + up_shape[2:], kind)] * UP_CHUNKS + [
         pltpu.VMEM((4,) + down_shape[2:], kind)
-    ] * CHUNKS
-    total = 2 * CHUNKS
+    ] * DOWN_CHUNKS
+    total = CHUNKS
     dma = pltpu.SemaphoreType.DMA
     block = (tok_count, half)
     by_spot = outs.reshape(4, 4, 2, tok_count, half).transpose(1, 0, 2, 3, 4)

time: 189 us -> 193 us (1.021)
  Pallas kernels: 154 us -> 158 us
    pallas_call x1, Pallas kernels: 114 us -> 118 us  [swap_and_return(): pl.pallas_call(swap_kernel, out_shape=(jax.ShapeDtypeStruct(up_shape, kin...]
where the time goes in v4:
time: 193 us
  Pallas kernels  158 us (82%)
  matrix products  18.1 us (9%)
  local copies, waits for them, and re-layouts  11.1 us (6%)
  other arithmetic  2.87 us (1%)
    pallas_call x1, Pallas kernels, swap_and_return(): pl.pallas_call(swap_kernel, out_shape=(jax.ShapeDtypeStruct(up_shape, kin...  118 us
    pallas_call x1, Pallas kernels, gather_tokens(): pl.pallas_call(gather_kernel, out_shape=(full, full, jax.ShapeDtypeStruct...  40.2 us
    unnamed x21, local copies, waits for them, and re-layouts  7.78 us
    dot_general x1, matrix products, dense_body(): lax.dot_general(rows, pre_grad, (((0,), (0,)), ((), ())), preferred_eleme...  5.68 us
    dot_general x1, matrix products, dense_body(): lax.dot_general(hidden, grads, (((0,), (0,)), ((), ())), preferred_elemen...  4.46 us
  transfers between devices with their start and end apart: 2, of which 1 were waited for; matrix products, arithmetic and copies ran while one was open for 4% of the time, Pallas kernels for 0%

profile of v4, /device:TPU:0, one launch (start us, length us, event | category | flops | bytes accessed | tf_op | source)
XLA Modules:
  0.0 192.7 jit_solution(5956604500024020934)
XLA Ops:
  0.6 0.0 copy-start
  0.7 0.8 iota_compare_fusion.1
  1.5 0.7 select_reduce_fusion.2
  2.2 0.1 select_reduce_fusion.1
  2.3 0.1 reshape.94
  2.4 1.0 bitcast_bitcast_fusion
  3.4 40.2 %shard_map.121 = (bf16[16,2,24,1024]{3,2,1,0:T(8,128)(2,1)S(1)}, bf16[16,2,24,1024]{3,2,1,0:T(8,128)(2,1)S(1)}, f32[16,2,8,128]{3,2,1,0:T(8,128)S(1)}) custom-call(bf16[2,24,1024]{2,1,0:T(8,128)(2,1)S(1)} %get-tuple-element.30.refs_0_, bf16[2,24,1024]{2,1,0:T(8,128)(2,1)S(1)} %get-tuple-element.29.refs_1_, f32[8,128]{1,0:T(8,128)S(1)} %pad.4.refs_2_), custom_call_target="tpu_custom_call" | custom-call | tf_op jit(solution)/shard_map/pallas_call | solution.py:567
  43.6 0.0 copy-start.1
  43.6 1.1 copy-done.1
  44.7 0.2 reshape.96
  44.9 0.1 select_reduce_fusion
  45.0 0.3 multiply_convert_fusion.1
  45.4 0.0 copy-done
  45.4 0.0 copy-start.2
  45.4 0.0 copy-start.6
  45.4 2.4 %fusion.8 = bf16[768,768]{1,0:T(8,128)(2,1)} fusion(bf16[768,1024]{1,0:T(8,128)(2,1)S(1)} %bitcast.60, bf16[1,768,1024]{2,1,0:T(8,128)(2,1)S(1)} %copy-done), kind=kOutput, calls=%fused_computation.19 | convolution fusion | flops 1208549376 | bytes 4325376 | tf_op jit(solution)/shard_map/dot_general | solution.py:610
  47.9 0.0 collective-permute-start
  47.9 0.0 copy-done.2
  47.9 0.0 copy-done.6
  47.9 0.0 copy-start.5
  47.9 2.4 %fusion.11 = bf16[768,768]{1,0:T(8,128)(2,1)} fusion(bf16[768,1024]{1,0:T(8,128)(2,1)S(1)} %bitcast.52, bf16[1,1024,768]{2,1,0:T(8,128)(2,1)S(1)} %copy-done.6), kind=kOutput, calls=%fused_computation.20 | convolution fusion | flops 1208549376 | bytes 4325376 | tf_op jit(solution)/shard_map/dot_general | solution.py:609
  50.3 0.5 collective-permute-start.1
  50.8 0.0 copy-done.5
  50.8 0.1 reshape.102
  50.9 0.2 reduce_window_sum.11
  51.1 0.1 mul.91
  51.2 0.1 sub.39
  51.3 0.1 select_reduce_fusion.3
  51.4 0.1 and_select_fusion.4
  51.5 0.6 concatenate.3.refs_0_
  52.1 0.3 fusion
  52.4 1.2 collective-permute-done.1
  53.6 3.1 %multiply_convert_fusion = bf16[768,1024]{1,0:T(8,128)(2,1)S(1)} fusion(f32[768]{0:T(1024)S(1)} %mul.91, bf16[1,768,1024]{2,1,0:T(8,128)(2,1)S(1)} %copy-done, bf16[768,768]{1,0:T(8,128)(2,1)} %collective-permute-done.1, bf16[768,768]{1,0:T(8,128)(2,1)} %fusion.11), kind=kOutput, calls=%fused_computation.6 | convolution fusion | flops 1215823872 | bytes 5508096 | tf_op jit(solution)/shard_map/dot_general | solution.py:633
  56.8 0.0 copy-start.3
  56.8 0.0 copy-start.7
  56.8 1.3 copy.28
  58.1 0.0 copy-start.8
  58.1 0.0 collective-permute-done
  58.1 0.7 copy-done.3
  58.7 0.5 copy-done.7
  59.2 5.7 %fusion.2 = bf16[1024,768]{1,0:T(8,128)(2,1)} fusion(bf16[1,1024,768]{2,1,0:T(8,128)(2,1)S(1)} %copy-done.7, bf16[768,1024]{1,0:T(8,128)(2,1)S(1)} %bitcast.53, bf16[768,768]{1,0:T(8,128)(2,1)} %collective-permute-done, bf16[768,768]{1,0:T(8,128)(2,1)} %fusion.8, bf16[768,768]{1,0:T(8,128)(2,1)} %collective-permute-done.1, bf16[768,768]{1,0:T(8,128)(2,1)} %fusion.11), kind=kOutput, calls=%fused_computation.5 | convolution fusion | flops 1220739072 | bytes 9437184 | tf_op jit(solution)/shard_map/dot_general | solution.py:621
  64.9 0.0 copy-done.8
  64.9 4.5 %fusion.1 = bf16[768,1024]{1,0:T(8,128)(2,1)} fusion(bf16[1,768,1024]{2,1,0:T(8,128)(2,1)S(1)} %copy-done.8, bf16[768,1024]{1,0:T(8,128)(2,1)S(1)} %fusion, bf16[768,768]{1,0:T(8,128)(2,1)} %collective-permute-done.1, bf16[768,768]{1,0:T(8,128)(2,1)} %fusion.11), kind=kOutput, calls=%fused_computation.3 | convolution fusion | flops 1216610304 | bytes 7077888 | tf_op jit(solution)/shard_map/dot_general | solution.py:627
  69.3 117.9 %shard_map.122 = (bf16[4,8,32,768]{3,2,1,0:T(8,128)(2,1)}, bf16[4,6,32,1024]{3,2,1,0:T(8,128)(2,1)}, bf16[24,2048]{1,0:T(8,128)(2,1)}) custom-call(s32[24]{0:T(128)} %concatenate.3.refs_0_, bf16[4,8,32,768]{3,2,1,0:T(8,128)(2,1)} %bitcast.55, bf16[4,6,32,1024]{3,2,1,0:T(8,128)(2,1)} %bitcast.56, bf16[4,4,2,24,1024]{4,3,2,1,0:T(8,128)(2,1)} %bitcast.54), custom_call_target="tpu_custom_call" | custom-call | tf_op jit(solution)/shard_map/pallas_call | solution.py:418
  187.2 1.5 copy.32
  188.8 0.0 copy-start.4
  188.8 2.8 %copy.33 = bf16[1,1024,768]{2,1,0:T(8,128)(2,1)} copy(bf16[1,1024,768]{2,1,0:T(8,128)(2,1)} %bitcast.58) | data formatting | bytes 3145728
  191.5 0.0 copy-done.4
  191.5 1.1 copy.34
  (8 shorter events, 0.1 us)
Async XLA Ops:
  0.6 44.7 %copy-start = (bf16[1,768,1024]{2,1,0:T(8,128)(2,1)S(1)}, bf16[1,768,1024]{2,1,0:T(8,128)(2,1)}, u32[]{:S(2)}) copy-start(bf16[1,768,1024]{2,1,0:T(8,128)(2,1)} %param.17) | copy-start | bytes 4718596
  43.6 1.1 copy-start.1
  45.4 2.5 %copy-start.2 = (bf16[16,2,24,1024]{3,2,1,0:T(8,128)(2,1)S(1)}, bf16[16,2,24,1024]{3,2,1,0:T(8,128)(2,1)}, u32[]{:S(2)}) copy-start(bf16[16,2,24,1024]{3,2,1,0:T(8,128)(2,1)} %copy-done.1) | copy-start | bytes 4718596
  45.4 2.5 %copy-start.6 = (bf16[1,1024,768]{2,1,0:T(8,128)(2,1)S(1)}, bf16[1,1024,768]{2,1,0:T(8,128)(2,1)}, u32[]{:S(2)}) copy-start(bf16[1,1024,768]{2,1,0:T(8,128)(2,1)} %param.16) | copy-start | bytes 4718596
  47.9 10.2 %collective-permute-start = (bf16[768,768]{1,0:T(8,128)(2,1)}, bf16[768,768]{1,0:T(8,128)(2,1)}, u32[]{:S(2)}, u32[]{:S(2)}) collective-permute-start(bf16[768,768]{1,0:T(8,128)(2,1)} %fusion.8), channel_id=1, source_target_pairs={{0,1},{1,0},{2,3},{3,2},{4,5},{5,4},{6,7},{7,6},{8,9},{9,8},{10,11... | collective-permute-start | bytes 3538952 | tf_op jit(solution)/shard_map/ppermute | solution.py:616
  47.9 2.9 %copy-start.5 = (s32[16]{0:T(128)S(1)}, s32[16]{0:T(128)}, u32[]{:S(2)}) copy-start(s32[16]{0:T(128)} %param.15) | copy-start | bytes 196
  50.3 3.3 %collective-permute-start.1 = (bf16[768,768]{1,0:T(8,128)(2,1)}, bf16[768,768]{1,0:T(8,128)(2,1)}, u32[]{:S(2)}, u32[]{:S(2)}) collective-permute-start(bf16[768,768]{1,0:T(8,128)(2,1)} %fusion.11), channel_id=1, source_target_pairs={{0,1},{1,0},{2,3},{3,2},{4,5},{5,4},{6,7},{7,6},{8,9},{9,8},{10,11... | collective-permute-start | bytes 3538952 | tf_op jit(solution)/shard_map/ppermute | solution.py:613
  56.8 2.0 %copy-start.3 = (bf16[16,2,24,1024]{3,2,1,0:T(8,128)(2,1)S(1)}, bf16[16,2,24,1024]{3,2,1,0:T(8,128)(2,1)}, u32[]{:S(2)}) copy-start(bf16[16,2,24,1024]{3,2,1,0:T(8,128)(2,1)} %copy-done.1) | copy-start | bytes 4718596
  56.8 2.4 %copy-start.7 = (bf16[1,1024,768]{2,1,0:T(8,128)(2,1)S(1)}, bf16[1,1024,768]{2,1,0:T(8,128)(2,1)}, u32[]{:S(2)}) copy-start(bf16[1,1024,768]{2,1,0:T(8,128)(2,1)} %param.18) | copy-start | bytes 4718596
  58.1 6.8 %copy-start.8 = (bf16[1,768,1024]{2,1,0:T(8,128)(2,1)S(1)}, bf16[1,768,1024]{2,1,0:T(8,128)(2,1)}, u32[]{:S(2)}) copy-start(bf16[1,768,1024]{2,1,0:T(8,128)(2,1)} %param.19) | copy-start | bytes 4718596
  188.8 2.8 %copy-start.4 = (bf16[4,6,32,1024]{3,2,1,0:T(8,128)(2,1)S(1)}, bf16[4,6,32,1024]{3,2,1,0:T(8,128)(2,1)}, u32[]{:S(2)}) copy-start(bf16[4,6,32,1024]{3,2,1,0:T(8,128)(2,1)} %get-tuple-element.14) | copy-start | bytes 4718596
